TPU v7x, 512 devices: a whole 4x8x8 slice. The times are simulated.
512 devices in a mesh: wide: 32 (over z, y_hi, core), narrow: 16 (over y_lo, x).
Axes of the slice: x: 4, y: 8 (y_hi: 2, y_lo: 4; y = y_hi * 4 + y_lo), z: 8, core: 2. Of those that a mesh axis runs over, the one named last changes fastest.
Arguments:
- packet_prev: float32 [64, 512, 16, 128], P('wide', None, 'narrow'), may hold values from -6 to 6
- packet_curr: float32 [64, 512, 16, 128], P('wide', None, 'narrow'), may hold values from -6 to 6
- potential: float32 [64, 512, 16, 128], P('wide', None, 'narrow'), may hold values from -0.6 to 0.6
- damping: float32 [64, 32], P('wide'), may hold values from 0.5 to 1
- kinetic_radial: float32 [64, 64], replicated, may hold values from -0.5 to 0.5, as said below
- kinetic_bond: float32 [32, 32], replicated, may hold values from -0.5 to 0.5, as said below
- kinetic_bend: float32 [16, 16], replicated, may hold values from -0.5 to 0.5, as said below
- kinetic_twist: float32 [16, 16], replicated, may hold values from -0.5 to 0.5, as said below
- kinetic_torsion: float32 [16, 16], replicated, may hold values from -0.5 to 0.5, as said below
- kinetic_umbrella: float32 [8, 8], replicated, may hold values from -0.5 to 0.5, as said below
Outputs:
- packet_next: float32 [64, 512, 16, 128], P('wide', None, 'narrow')
- packet_last: float32 [64, 512, 16, 128], P('wide', None, 'narrow')
Inputs may be any that keep to these rules, and one draw needn't show every extreme that they name: `kinetic_radial`: symmetric. `kinetic_bond`: symmetric. `kinetic_bend`: symmetric. `kinetic_twist`: symmetric. `kinetic_torsion`: symmetric. `kinetic_umbrella`: symmetric.
All inputs are finite; a program needn't handle non-finite values.
Results may differ from a plain program's by a relative error of at most 0.0001.
Values sent between devices are 32-bit elements; how exact they have to be, the bound alone decides.
No kernel may reach another device: no remote copies, remote signals or barrier semaphores. Data moves between devices by JAX's collectives and lax.ppermute only.
A program may use at most 64 MiB of HBM per device.

v0:
```python
import jax
import jax.numpy as jnp
from jax import lax
from jax.sharding import PartitionSpec as P


def kronecker_sum(matrix_left, matrix_right):
    left_count = matrix_left.shape[0]
    right_count = matrix_right.shape[0]
    identity_left = jnp.eye(left_count, dtype=jnp.float32)
    identity_right = jnp.eye(right_count, dtype=jnp.float32)
    first_part = matrix_left[:, None, :, None] * identity_right[None, :, None, :]
    second_part = identity_left[:, None, :, None] * matrix_right[None, :, None, :]
    return (first_part + second_part).reshape(left_count * right_count, left_count * right_count)


def local(
    packet_prev,
    packet_curr,
    potential,
    damping,
    kinetic_radial,
    kinetic_bond,
    kinetic_bend,
    kinetic_twist,
    kinetic_torsion,
    kinetic_umbrella,
):
    highest = lax.Precision.HIGHEST
    row_count, inner_size, slab_count, column_count = packet_curr.shape
    bond_count = kinetic_bond.shape[0]
    bend_count = kinetic_bend.shape[0]
    inner_matrix = kronecker_sum(kinetic_bond, kinetic_bend)
    outer_matrix = kronecker_sum(kinetic_torsion, kinetic_umbrella)
    damping_full = jnp.broadcast_to(
        damping[:, :, None], (row_count, bond_count, bend_count)
    ).reshape(row_count, inner_size)[:, :, None, None]

    def local_part(packet):
        total = jnp.einsum("ij,ajbc->aibc", inner_matrix, packet, precision=highest)
        total = total + jnp.einsum("abcj,ij->abci", packet, outer_matrix, precision=highest)
        return total + potential * packet

    def along_radial(block):
        return jnp.einsum("ij,jabc->iabc", kinetic_radial, block, precision=highest)

    def along_twist(block):
        return jnp.einsum("ij,abjc->abic", kinetic_twist, block, precision=highest)

    def apply_hamiltonian(packet):
        radial_term = along_radial(
            lax.all_to_all(packet, "wide", split_axis=1, concat_axis=0, tiled=True)
        )
        remote_part = lax.all_to_all(radial_term, "wide", split_axis=0, concat_axis=1, tiled=True)
        twist_term = along_twist(
            lax.all_to_all(packet, "narrow", split_axis=1, concat_axis=2, tiled=True)
        )
        remote_part = remote_part + lax.all_to_all(
            twist_term, "narrow", split_axis=2, concat_axis=1, tiled=True
        )
        return local_part(packet) + remote_part

    next_term = damping_full * (2.0 * apply_hamiltonian(packet_curr) - damping_full * packet_prev)
    last_term = damping_full * (2.0 * apply_hamiltonian(next_term) - damping_full * packet_curr)
    return (next_term, last_term)


def solution(mesh):
    placed = (
        P("wide", None, "narrow", None),
        P("wide", None, "narrow", None),
        P("wide", None, "narrow", None),
        P("wide", None),
        P(),
        P(),
        P(),
        P(),
        P(),
        P(),
    )
    return jax.shard_map(
        local,
        mesh=mesh,
        in_specs=placed,
        out_specs=(P("wide", None, "narrow", None), P("wide", None, "narrow", None)),
        check_vma=False,
    )
```

profile of v0, /device:TPU:8, one launch (start us, length us, event | category | flops | bytes accessed | tf_op | source)
XLA Modules:
  0.0 209.3 jit_solution(3178556084836599280)
XLA Ops:
  0.7 2.3 %copy.81 = f32[2,512,1,128]{3,0,2,1:T(2,128)} copy(f32[2,512,1,128]{3,2,1,0:T(1,128)} %param.11) | data formatting | bytes 1048576 | tf_op args[1]
  2.9 9.2 %all-to-all-start.2 = ((f32[2,512,1,128]{3,0,2,1:T(2,128)}), f32[2,512,1,128]{3,0,2,1:T(2,128)S(1)}, u32[]{:S(2)}, u32[]{:S(2)}) async-start(f32[2,512,1,128]{3,0,2,1:T(2,128)} %copy.81), calls=%async_computation.2 | async-start | bytes 1048576 | tf_op jit(solution)/shard_map/all_to_all | solution.py:56
  12.1 2.2 %copy.77 = f32[2,512,1,128]{3,2,0,1:T(1,128)} copy(f32[2,512,1,128]{3,2,1,0:T(1,128)} %param.11) | data formatting | bytes 1048576 | tf_op args[1]
  14.3 11.2 %all-to-all-done.2 = f32[2,512,1,128]{3,0,2,1:T(2,128)S(1)} async-done(((f32[2,512,1,128]{3,0,2,1:T(2,128)}), f32[2,512,1,128]{3,0,2,1:T(2,128)S(1)}, u32[]{:S(2)}, u32[]{:S(2)}) %all-to-all-start.2) | async-done | bytes 524320 | tf_op jit(solution)/shard_map/all_to_all | solution.py:56
  25.6 13.2 %all-to-all-start = ((f32[2,512,1,128]{3,2,0,1:T(1,128)}), f32[2,512,1,128]{3,2,0,1:T(1,128)S(1)}, u32[]{:S(2)}, u32[]{:S(2)}) async-start(f32[2,512,1,128]{3,2,0,1:T(1,128)} %copy.77), calls=%async_computation | async-start | bytes 1048576 | tf_op jit(solution)/shard_map/all_to_all | solution.py:52
  38.8 1.6 convolution_bitcast_fusion.4
  41.3 20.1 %all-to-all-done = f32[2,512,1,128]{3,2,0,1:T(1,128)S(1)} async-done(((f32[2,512,1,128]{3,2,0,1:T(1,128)}), f32[2,512,1,128]{3,2,0,1:T(1,128)S(1)}, u32[]{:S(2)}, u32[]{:S(2)}) %all-to-all-start) | async-done | bytes 524320 | tf_op jit(solution)/shard_map/all_to_all | solution.py:52
  61.4 4.6 %all-to-all-start.3 = ((f32[2,32,16,128]{3,1,0,2:T(8,128)}), f32[2,32,16,128]{3,1,0,2:T(8,128)S(1)}, u32[]{:S(2)}, u32[]{:S(2)}) async-start(f32[2,32,16,128]{3,1,0,2:T(8,128)} %copy.84), calls=%async_computation.3 | async-start | bytes 1048576 | tf_op jit(solution)/shard_map/all_to_all | solution.py:58
  68.0 12.0 %all-to-all-done.3 = f32[2,32,16,128]{3,1,0,2:T(8,128)S(1)} async-done(((f32[2,32,16,128]{3,1,0,2:T(8,128)}), f32[2,32,16,128]{3,1,0,2:T(8,128)S(1)}, u32[]{:S(2)}, u32[]{:S(2)}) %all-to-all-start.3) | async-done | bytes 524320 | tf_op jit(solution)/shard_map/all_to_all | solution.py:58
  80.0 4.6 %all-to-all-start.1 = ((f32[64,16,1,128]{3,1,2,0:T(8,128)}), f32[64,16,1,128]{3,1,2,0:T(8,128)}, u32[]{:S(2)}, u32[]{:S(2)}) async-start(f32[64,16,1,128]{3,1,2,0:T(8,128)} %copy.79), calls=%async_computation.1 | async-start | bytes 1048576 | tf_op jit(solution)/shard_map/all_to_all | solution.py:54
  84.7 4.6 %multiply_add_fusion = f32[32,16,32,16]{3,2,1,0:T(8,128)} fusion(f32[16,16]{1,0:T(8,128)S(1)} %copy-done.9, f32[32,32]{1,0:T(8,128)S(1)} %fusion.20, f32[16,16]{1,0:T(8,128)S(1)} %fusion.23, f32[32,32]{1,0:T(8,128)S(1)} %copy-done.7), kind=kLoop, calls=%fused_computation | loop fusion | flops 786432 | bytes 1058816 | tf_op jit(solution)/shard_map/add | solution.py:14
  89.3 7.7 %reshape.160 = f32[512,512,1]{1,0,2:T(8,128)S(1)} reshape(f32[32,16,32,16]{3,2,1,0:T(8,128)} %multiply_add_fusion) | data formatting | bytes 2097152 | tf_op jit(solution)/shard_map/add | solution.py:14
  100.0 7.3 %all-to-all-done.1 = f32[64,16,1,128]{3,1,2,0:T(8,128)} async-done(((f32[64,16,1,128]{3,1,2,0:T(8,128)}), f32[64,16,1,128]{3,1,2,0:T(8,128)}, u32[]{:S(2)}, u32[]{:S(2)}) %all-to-all-start.1) | async-done | bytes 524320 | tf_op jit(solution)/shard_map/all_to_all | solution.py:54
  108.4 1.7 fusion.5
  111.3 18.6 %all_to_all.138 = f32[2,512,1,128]{3,0,2,1:T(2,128)} all-to-all(f32[2,512,1,128]{3,0,2,1:T(2,128)} %copy.90), channel_id=1, replica_groups=mesh['wide'=32,'narrow'=16] {'narrow'}, dimensions={1} | all-to-all | bytes 1048576 | tf_op jit(solution)/shard_map/all_to_all | solution.py:56
  129.9 6.7 %all-to-all-start.4 = ((f32[2,512,1,128]{3,0,2,1:T(2,128)}), f32[2,512,1,128]{3,0,2,1:T(2,128)S(1)}, u32[]{:S(2)}, u32[]{:S(2)}) async-start(f32[2,512,1,128]{3,0,2,1:T(2,128)} %copy.90), calls=%async_computation.4 | async-start | bytes 1048576 | tf_op jit(solution)/shard_map/all_to_all | solution.py:52
  136.6 1.9 convolution_bitcast_fusion
  139.5 19.6 %all-to-all-done.4 = f32[2,512,1,128]{3,0,2,1:T(2,128)S(1)} async-done(((f32[2,512,1,128]{3,0,2,1:T(2,128)}), f32[2,512,1,128]{3,0,2,1:T(2,128)S(1)}, u32[]{:S(2)}, u32[]{:S(2)}) %all-to-all-start.4) | async-done | bytes 524320 | tf_op jit(solution)/shard_map/all_to_all | solution.py:52
  159.9 4.6 %all-to-all-start.7 = ((f32[2,32,16,128]{3,1,0,2:T(8,128)}), f32[2,32,16,128]{3,1,0,2:T(8,128)S(1)}, u32[]{:S(2)}, u32[]{:S(2)}) async-start(f32[2,32,16,128]{3,1,0,2:T(8,128)} %copy.97), calls=%async_computation.7 | async-start | bytes 1048576 | tf_op jit(solution)/shard_map/all_to_all | solution.py:58
  167.5 10.9 %all-to-all-done.7 = f32[2,32,16,128]{3,1,0,2:T(8,128)S(1)} async-done(((f32[2,32,16,128]{3,1,0,2:T(8,128)}), f32[2,32,16,128]{3,1,0,2:T(8,128)S(1)}, u32[]{:S(2)}, u32[]{:S(2)}) %all-to-all-start.7) | async-done | bytes 524320 | tf_op jit(solution)/shard_map/all_to_all | solution.py:58
  178.4 4.6 %all-to-all-start.5 = ((f32[64,16,1,128]{3,1,2,0:T(8,128)}), f32[64,16,1,128]{3,1,2,0:T(8,128)}, u32[]{:S(2)}, u32[]{:S(2)}) async-start(f32[64,16,1,128]{3,1,2,0:T(8,128)} %copy.92), calls=%async_computation.5 | async-start | bytes 1048576 | tf_op jit(solution)/shard_map/all_to_all | solution.py:54
  183.0 1.8 convolution_bitcast_fusion.3
  184.9 20.8 %all-to-all-done.5 = f32[64,16,1,128]{3,1,2,0:T(8,128)} async-done(((f32[64,16,1,128]{3,1,2,0:T(8,128)}), f32[64,16,1,128]{3,1,2,0:T(8,128)}, u32[]{:S(2)}, u32[]{:S(2)}) %all-to-all-start.5) | async-done | bytes 524320 | tf_op jit(solution)/shard_map/all_to_all | solution.py:54
  206.8 2.5 %fusion.11 = f32[2,512,1,128]{3,1,0,2:T(8,128)} fusion(f32[2,512,1,128]{3,1,0,2:T(8,128)S(1)} %bitcast_add_fusion, f32[2,512,1,128]{3,1,0,2:T(8,128)} %convolution_bitcast_fusion.3, f32[128,128,1]{1,0,2:T(8,128)S(1)} %reshape.161, f32[2,512,1,128]{3,1,0,2:T(8,128)S(1)} %fusion.5, f32[2,512,1,128]{3,1,0,2:T(8,128)S(1)} %bitcast.130, ...), kind=kOutput, calls=%fused_computation.20 | convolution fusion | flops 202375168 | bytes 3215360 | tf_op jit(solution)/shard_map/abcj,ij->abci/dot_general | solution.py:41
  (47 shorter events, 14.1 us)
Async XLA Ops:
  0.6 65.7 %copy-start = (f32[64,64]{1,0:T(8,128)S(1)}, f32[64,64]{1,0:T(8,128)}, u32[]{:S(2)}) copy-start(f32[64,64]{1,0:T(8,128)} %param.14) | copy-start | bytes 49156
  0.6 84.0 %copy-start.7 = (f32[32,32]{1,0:T(8,128)S(1)}, f32[32,32]{1,0:T(8,128)}, u32[]{:S(2)}) copy-start(f32[32,32]{1,0:T(8,128)} %param.15) | copy-start | bytes 12292
  0.7 84.0 %copy-start.9 = (f32[16,16]{1,0:T(8,128)S(1)}, f32[16,16]{1,0:T(8,128)}, u32[]{:S(2)}) copy-start(f32[16,16]{1,0:T(8,128)} %param.16) | copy-start | bytes 3076
  2.9 22.6 %all-to-all-start.2 = ((f32[2,512,1,128]{3,0,2,1:T(2,128)}), f32[2,512,1,128]{3,0,2,1:T(2,128)S(1)}, u32[]{:S(2)}, u32[]{:S(2)}) async-start(f32[2,512,1,128]{3,0,2,1:T(2,128)} %copy.81), calls=%async_computation.2 | async-start | bytes 1048576 | tf_op jit(solution)/shard_map/all_to_all | solution.py:56
  25.6 35.8 %all-to-all-start = ((f32[2,512,1,128]{3,2,0,1:T(1,128)}), f32[2,512,1,128]{3,2,0,1:T(1,128)S(1)}, u32[]{:S(2)}, u32[]{:S(2)}) async-start(f32[2,512,1,128]{3,2,0,1:T(1,128)} %copy.77), calls=%async_computation | async-start | bytes 1048576 | tf_op jit(solution)/shard_map/all_to_all | solution.py:52
  61.4 18.5 %all-to-all-start.3 = ((f32[2,32,16,128]{3,1,0,2:T(8,128)}), f32[2,32,16,128]{3,1,0,2:T(8,128)S(1)}, u32[]{:S(2)}, u32[]{:S(2)}) async-start(f32[2,32,16,128]{3,1,0,2:T(8,128)} %copy.84), calls=%async_computation.3 | async-start | bytes 1048576 | tf_op jit(solution)/shard_map/all_to_all | solution.py:58
  80.0 4.6 %copy-start.4 = (f32[2,32,16,128]{3,1,0,2:T(8,128)}, f32[2,32,16,128]{3,1,0,2:T(8,128)S(1)}, u32[]{:S(2)}) copy-start(f32[2,32,16,128]{3,1,0,2:T(8,128)S(1)} %all-to-all-done.3) | copy-start | bytes 1572868
  80.0 27.3 %all-to-all-start.1 = ((f32[64,16,1,128]{3,1,2,0:T(8,128)}), f32[64,16,1,128]{3,1,2,0:T(8,128)}, u32[]{:S(2)}, u32[]{:S(2)}) async-start(f32[64,16,1,128]{3,1,2,0:T(8,128)} %copy.79), calls=%async_computation.1 | async-start | bytes 1048576 | tf_op jit(solution)/shard_map/all_to_all | solution.py:54
  84.6 12.4 %copy-start.8 = (f32[16,16]{1,0:T(8,128)S(1)}, f32[16,16]{1,0:T(8,128)}, u32[]{:S(2)}) copy-start(f32[16,16]{1,0:T(8,128)} %param.18) | copy-start | bytes 3076
  84.6 12.4 %copy-start.10 = (f32[8,8]{1,0:T(8,128)S(1)}, f32[8,8]{1,0:T(8,128)}, u32[]{:S(2)}) copy-start(f32[8,8]{1,0:T(8,128)} %param.19) | copy-start | bytes 772
  84.6 13.1 %copy-start.11 = (f32[2,32]{1,0:T(2,128)S(1)}, f32[2,32]{1,0:T(2,128)}, u32[]{:S(2)}) copy-start(f32[2,32]{1,0:T(2,128)} %param.13) | copy-start | bytes 772
  84.7 13.2 %copy-start.1 = (f32[2,512,1,128]{3,2,1,0:T(1,128)S(1)}, f32[2,512,1,128]{3,2,1,0:T(1,128)}, u32[]{:S(2)}) copy-start(f32[2,512,1,128]{3,2,1,0:T(1,128)} %param.11) | copy-start | bytes 1572868
  89.3 19.1 %copy-start.3 = (f32[2,512,1,128]{3,2,1,0:T(1,128)S(1)}, f32[2,512,1,128]{3,2,1,0:T(1,128)}, u32[]{:S(2)}) copy-start(f32[2,512,1,128]{3,2,1,0:T(1,128)} %param.12) | copy-start | bytes 1572868
  97.0 39.7 %copy-start.6 = (f32[16,16]{1,0:T(8,128)S(1)}, f32[16,16]{1,0:T(8,128)}, u32[]{:S(2)}) copy-start(f32[16,16]{1,0:T(8,128)} %param.17) | copy-start | bytes 3076
  110.1 99.2 %copy-start.2 = (f32[2,512,1,128]{3,1,0,2:T(8,128)}, f32[2,512,1,128]{3,1,0,2:T(8,128)S(1)}, u32[]{:S(2)}) copy-start(f32[2,512,1,128]{3,1,0,2:T(8,128)S(1)} %fusion.5) | copy-start | bytes 1572868
  129.9 29.2 %all-to-all-start.4 = ((f32[2,512,1,128]{3,0,2,1:T(2,128)}), f32[2,512,1,128]{3,0,2,1:T(2,128)S(1)}, u32[]{:S(2)}, u32[]{:S(2)}) async-start(f32[2,512,1,128]{3,0,2,1:T(2,128)} %copy.90), calls=%async_computation.4 | async-start | bytes 1048576 | tf_op jit(solution)/shard_map/all_to_all | solution.py:52
  159.1 0.8 copy-start.5
  159.9 18.5 %all-to-all-start.7 = ((f32[2,32,16,128]{3,1,0,2:T(8,128)}), f32[2,32,16,128]{3,1,0,2:T(8,128)S(1)}, u32[]{:S(2)}, u32[]{:S(2)}) async-start(f32[2,32,16,128]{3,1,0,2:T(8,128)} %copy.97), calls=%async_computation.7 | async-start | bytes 1048576 | tf_op jit(solution)/shard_map/all_to_all | solution.py:58
  178.4 27.3 %all-to-all-start.5 = ((f32[64,16,1,128]{3,1,2,0:T(8,128)}), f32[64,16,1,128]{3,1,2,0:T(8,128)}, u32[]{:S(2)}, u32[]{:S(2)}) async-start(f32[64,16,1,128]{3,1,2,0:T(8,128)} %copy.92), calls=%async_computation.5 | async-start | bytes 1048576 | tf_op jit(solution)/shard_map/all_to_all | solution.py:54
where the time goes:
time: 211 us; the launch traced here: 209 us
  waiting for transfers between devices  102 us (48%)
  starting transfers between devices  47.6 us (23%)
  local copies, waits for them, and re-layouts  23.8 us (11%)
  blocking collectives  18.6 us (9%)
  matrix products  11.6 us (5%)
  other arithmetic  4.95 us (2%)
    all_to_all x2, waiting for transfers between devices, apply_hamiltonian(): lax.all_to_all(packet, 'wide', split_axis=1, concat_axis=0, tiled=True)  39.7 us
    all_to_all x2, waiting for transfers between devices, apply_hamiltonian(): lax.all_to_all(radial_term, 'wide', split_axis=0, concat_axis=1, tiled=True)  28.1 us
    all_to_all x2, waiting for transfers between devices, apply_hamiltonian(): lax.all_to_all(twist_term, 'narrow', split_axis=2, concat_axis=1, tiled=T...  22.8 us
    all_to_all x2, starting transfers between devices, apply_hamiltonian(): lax.all_to_all(packet, 'wide', split_axis=1, concat_axis=0, tiled=True)  19.9 us
    all_to_all x1, blocking collectives, apply_hamiltonian(): lax.all_to_all(packet, 'narrow', split_axis=1, concat_axis=2, tiled=True)  18.6 us
    all_to_all x1, waiting for transfers between devices, apply_hamiltonian(): lax.all_to_all(packet, 'narrow', split_axis=1, concat_axis=2, tiled=True)  11.2 us
    all_to_all x2, starting transfers between devices, apply_hamiltonian(): lax.all_to_all(twist_term, 'narrow', split_axis=2, concat_axis=1, tiled=T...  9.24 us
    all_to_all x2, starting transfers between devices, apply_hamiltonian(): lax.all_to_all(radial_term, 'wide', split_axis=0, concat_axis=1, tiled=True)  9.24 us
  transfers between devices with their start and end apart: 7, of which 7 were waited for; matrix products, arithmetic and copies ran while one was open for 14% of the time, Pallas kernels for 0%

commit v1 on v0

v1 whole, which is shorter than its diff:
```python
import jax
import jax.numpy as jnp
from jax import lax
from jax.experimental import pallas as pl
from jax.experimental.pallas import tpu as pltpu
from jax.sharding import PartitionSpec as P

AXES = ("narrow", "wide")
F32 = jnp.float32
BF16 = jnp.bfloat16


def exact_dot(left, right):
    return jnp.dot(left, right, precision=lax.Precision.HIGHEST, preferred_element_type=F32)


def dot(left, right):
    return jnp.dot(left, right, preferred_element_type=F32)


def split(value):
    high = value.astype(BF16)
    return high, (value - high.astype(F32)).astype(BF16)


def iota(shape, axis):
    return lax.broadcasted_iota(jnp.int32, shape, axis)


def ones_where(condition):
    return jnp.where(condition, 1.0, 0.0).astype(F32)


def build_inner(bond_ref, bend_ref, high_ref, low_ref):
    bonds, bends = bond_ref.shape[0], bend_ref.shape[0]
    size = bonds * bends
    spread_bond = exact_dot(bond_ref[...], ones_where(iota((bonds, size), 0) == iota((bonds, size), 1) // bends))
    spread_bend = exact_dot(bend_ref[...], ones_where(iota((bends, size), 0) == iota((bends, size), 1) % bends))
    same_bend = iota((bends, size), 0) == iota((bends, size), 1) % bends
    bond_of = iota((bends, size), 1) // bends
    for bond in range(bonds):
        row = jnp.broadcast_to(spread_bond[bond : bond + 1, :], (bends, size))
        block = jnp.where(same_bend, row, 0.0) + jnp.where(bond_of == bond, spread_bend, 0.0)
        high, low = split(block)
        high_ref[pl.ds(bond * bends, bends), :] = high
        low_ref[pl.ds(bond * bends, bends), :] = low


def build_outer(torsion_ref, umbrella_ref):
    torsions, umbrellas = torsion_ref.shape[0], umbrella_ref.shape[0]
    size = torsions * umbrellas
    spread = ones_where(iota((torsions, size), 0) == iota((torsions, size), 1) // umbrellas)
    spread_rows = ones_where(iota((size, torsions), 1) == iota((size, torsions), 0) // umbrellas)
    tile = ones_where(iota((umbrellas, size), 0) == iota((umbrellas, size), 1) % umbrellas)
    tile_rows = ones_where(iota((size, umbrellas), 1) == iota((size, umbrellas), 0) % umbrellas)
    row, column = iota((size, size), 0), iota((size, size), 1)
    torsion = exact_dot(spread_rows, exact_dot(torsion_ref[...].T, spread))
    umbrella = exact_dot(tile_rows, exact_dot(umbrella_ref[...].T, tile))
    return jnp.where(row % umbrellas == column % umbrellas, torsion, 0.0) + jnp.where(
        row // umbrellas == column // umbrellas, umbrella, 0.0
    )


def damping_columns(damping_ref, size):
    slabs, bonds = damping_ref.shape
    bends = size // bonds
    owner = iota((size, bonds), 0) // bends == iota((size, bonds), 1)
    return [
        jnp.sum(
            jnp.where(owner, jnp.broadcast_to(damping_ref[slab : slab + 1, :], (size, bonds)), 0.0),
            axis=1,
            keepdims=True,
        )
        for slab in range(slabs)
    ]


def local_kinetic(fields, high_ref, low_ref, outer, rows):
    outer_high, outer_low = split(outer)
    outer_both = jnp.concatenate([outer_high, outer_high], axis=0)
    parts = [split(field) for field in fields]
    high = jnp.concatenate([part[0] for part in parts], axis=1)
    low = jnp.concatenate([part[1] for part in parts], axis=1)
    both = jnp.concatenate([high, low], axis=1)
    width = high.shape[1]
    lanes = fields[0].shape[1]
    results = []
    for start in range(0, fields[0].shape[0], rows):
        chunk = pl.ds(start, rows)
        product = dot(high_ref[chunk, :], both)
        inner = product[:, :width] + product[:, width:] + dot(low_ref[chunk, :], high)
        line = []
        for at, (part_high, part_low) in enumerate(parts):
            part_high, part_low = part_high[start : start + rows], part_low[start : start + rows]
            turned = dot(jnp.concatenate([part_high, part_low], axis=1), outer_both) + dot(part_high, outer_low)
            line.append(inner[:, at * lanes : (at + 1) * lanes] + turned)
        results.append(line)
    return results


ROWS = 128


def first_kernel(
    prev_ref, curr_ref, potential_ref, damping_ref, bond_ref, bend_ref, torsion_ref, umbrella_ref, message_ref, high_ref, low_ref
):
    slabs, size, lanes = curr_ref.shape
    build_inner(bond_ref, bend_ref, high_ref, low_ref)
    outer = build_outer(torsion_ref, umbrella_ref)
    damping = damping_columns(damping_ref, size)
    stride = 2 * slabs + 1
    fields = [curr_ref[slab] for slab in range(slabs)]
    kinetic = local_kinetic(fields, high_ref, low_ref, outer, ROWS)
    for at, line in enumerate(kinetic):
        start = at * ROWS
        chunk = slice(start, start + ROWS)
        for slab in range(slabs):
            field = fields[slab][chunk]
            total = line[slab] + potential_ref[slab, chunk] * field
            rest = 2.0 * total - damping[slab][chunk] * prev_ref[slab, chunk]
            message_ref[pl.ds(start * stride + slab, ROWS, stride=stride), :] = field
            message_ref[pl.ds(start * stride + slabs + slab, ROWS, stride=stride), :] = rest
        factors = jnp.where(iota((ROWS, lanes), 1) < lanes // 2, damping[0][chunk], damping[1][chunk])
        message_ref[pl.ds(start * stride + 2 * slabs, ROWS, stride=stride), :] = factors


def middle_kernel(slabs, message_ref, radial_ref, twist_ref, back_ref, high_ref, low_ref):
    lanes = message_ref.shape[1]
    radials, twists = radial_ref.shape[0], twist_ref.shape[0]
    groups = radials // slabs
    size = twists * groups
    stride = 2 * slabs + 1

    spread = exact_dot(twist_ref[...], ones_where(iota((twists, size), 0) == iota((twists, size), 1) // groups))
    same_group = iota((groups, size), 0) == iota((groups, size), 1) % groups
    for twist in range(twists):
        block = jnp.where(same_group, jnp.broadcast_to(spread[twist : twist + 1, :], (groups, size)), 0.0)
        high, low = split(block)
        high_ref[pl.ds(twist * groups, groups), :] = high
        low_ref[pl.ds(twist * groups, groups), :] = low

    order = ones_where(iota((radials, radials), 1) == (iota((radials, radials), 0) % groups) * slabs + iota((radials, radials), 0) // groups)
    order_back = ones_where(iota((radials, radials), 0) == (iota((radials, radials), 1) % groups) * slabs + iota((radials, radials), 1) // groups)
    radial_high, radial_low = split(exact_dot(exact_dot(order, radial_ref[...]), order_back))
    radial = jnp.concatenate([radial_high, radial_high, radial_low, radial_low], axis=1)

    def apply(fields):
        parts = [split(field) for field in fields]
        high = jnp.concatenate([part[0] for part in parts], axis=1)
        low = jnp.concatenate([part[1] for part in parts], axis=1)
        both = jnp.concatenate([high, low], axis=1)
        width = high.shape[1]
        outs = [[] for _ in range(slabs)]
        for twist in range(twists):
            rows = slice(twist * groups, (twist + 1) * groups)
            chunk = pl.ds(twist * groups, groups)
            stack = [part[0][rows] for part in parts] + [part[1][rows] for part in parts]
            along = dot(radial, jnp.concatenate(stack + stack, axis=0))
            product = dot(high_ref[chunk, :], both)
            across = product[:, :width] + product[:, width:] + dot(low_ref[chunk, :], high)
            for slab in range(slabs):
                outs[slab].append(along[slab * groups : (slab + 1) * groups] + across[:, slab * lanes : (slab + 1) * lanes])
        return [jnp.concatenate(out, axis=0) for out in outs]

    curr = [message_ref[pl.ds(slab, size, stride=stride), :] for slab in range(slabs)]
    turned = apply(curr)
    factors = message_ref[pl.ds(2 * slabs, size, stride=stride), :]
    following = []
    for slab in range(slabs):
        rest = message_ref[pl.ds(slabs + slab, size, stride=stride), :]
        place = slab * (lanes // 2)
        following.append(factors[:, place : place + 1] * (rest + 2.0 * turned[slab]))
    for slab, value in enumerate(following):
        back_ref[pl.ds(slab, size, stride=2 * slabs), :] = value
    for slab, value in enumerate(apply(following)):
        back_ref[pl.ds(slabs + slab, size, stride=2 * slabs), :] = value


def last_kernel(
    back_ref, curr_ref, potential_ref, damping_ref, bond_ref, bend_ref, torsion_ref, umbrella_ref, next_ref, last_ref, high_ref, low_ref
):
    slabs, size, _ = curr_ref.shape
    build_inner(bond_ref, bend_ref, high_ref, low_ref)
    outer = build_outer(torsion_ref, umbrella_ref)
    damping = damping_columns(damping_ref, size)
    stride = 2 * slabs
    fields = [back_ref[pl.ds(slab, size, stride=stride), :] for slab in range(slabs)]
    for slab in range(slabs):
        next_ref[slab] = fields[slab]
    kinetic = local_kinetic(fields, high_ref, low_ref, outer, ROWS)
    for at, line in enumerate(kinetic):
        start = at * ROWS
        chunk = slice(start, start + ROWS)
        for slab in range(slabs):
            remote = back_ref[pl.ds(start * stride + slabs + slab, ROWS, stride=stride), :]
            total = line[slab] + remote + potential_ref[slab, chunk] * fields[slab][chunk]
            factor = damping[slab][chunk]
            last_ref[slab, chunk] = factor * (2.0 * total - factor * curr_ref[slab, chunk])


PARAMS = pltpu.CompilerParams(vmem_limit_bytes=40 * 1024 * 1024)


def local(
    packet_prev,
    packet_curr,
    potential,
    damping,
    kinetic_radial,
    kinetic_bond,
    kinetic_bend,
    kinetic_twist,
    kinetic_torsion,
    kinetic_umbrella,
):
    slabs, size, _, lanes = packet_curr.shape
    flat = (slabs, size, lanes)
    inner = (kinetic_bond, kinetic_bend, kinetic_torsion, kinetic_umbrella)
    prev, curr, field = (value.reshape(flat) for value in (packet_prev, packet_curr, potential))
    scratch = [pltpu.VMEM((size, size), BF16), pltpu.VMEM((size, size), BF16)]
    stride = 2 * slabs + 1
    message = pl.pallas_call(
        first_kernel,
        out_shape=jax.ShapeDtypeStruct((size * stride, lanes), F32),
        scratch_shapes=scratch,
        compiler_params=PARAMS,
    )(prev, curr, field, damping, *inner)
    message = lax.all_to_all(
        message.reshape(size, stride, 1, lanes), AXES, split_axis=0, concat_axis=0, tiled=True
    ).reshape(size * stride, lanes)
    rows = kinetic_twist.shape[0] * (kinetic_radial.shape[0] // slabs)
    back = pl.pallas_call(
        lambda *refs: middle_kernel(slabs, *refs),
        out_shape=jax.ShapeDtypeStruct((rows * 2 * slabs, lanes), F32),
        scratch_shapes=[pltpu.VMEM((rows, rows), BF16), pltpu.VMEM((rows, rows), BF16)],
        compiler_params=PARAMS,
    )(message, kinetic_radial, kinetic_twist)
    back = lax.all_to_all(
        back.reshape(size, 2 * slabs, lanes), AXES, split_axis=0, concat_axis=0, tiled=True
    ).reshape(size * 2 * slabs, lanes)
    next_term, last_term = pl.pallas_call(
        last_kernel,
        out_shape=(jax.ShapeDtypeStruct(flat, F32), jax.ShapeDtypeStruct(flat, F32)),
        scratch_shapes=scratch,
        compiler_params=PARAMS,
    )(back, curr, field, damping, *inner)
    return next_term.reshape(packet_curr.shape), last_term.reshape(packet_curr.shape)


def solution(mesh):
    placed = (
        P("wide", None, "narrow", None),
        P("wide", None, "narrow", None),
        P("wide", None, "narrow", None),
        P("wide", None),
        P(),
        P(),
        P(),
        P(),
        P(),
        P(),
    )
    return jax.shard_map(
        local,
        mesh=mesh,
        in_specs=placed,
        out_specs=(P("wide", None, "narrow", None), P("wide", None, "narrow", None)),
        check_vma=False,
    )
```

time: 211 us -> 121 us (0.57)
  the two profiles are of different devices: /device:TPU:8 before, /device:TPU:1 now
where the time goes in v1:
time: 121 us; the launch traced here: 120 us
  blocking collectives  104 us (86%)
  Pallas kernels  8.69 us (7%)
  local copies, waits for them, and re-layouts  6.65 us (5%)
    all_to_all x1, blocking collectives, local(): lax.all_to_all(message.reshape(size, stride, 1, lanes), AXES, split_axis=...  60.4 us
    all_to_all x1, blocking collectives, local(): lax.all_to_all(back.reshape(size, 2 * slabs, lanes), AXES, split_axis=0,...  43.5 us
    unnamed x34, local copies, waits for them, and re-layouts  6.65 us
    pallas_call x1, Pallas kernels, local(): pl.pallas_call(lambda *refs: middle_kernel(slabs, *refs), out_shape=jax.S...  5.34 us

profile of v1, /device:TPU:1, one launch (start us, length us, event | category | flops | bytes accessed | tf_op | source)
XLA Modules:
  0.0 120.0 jit_solution(14317841853238452294)
XLA Ops:
  0.6 0.0 copy-start
  0.6 1.0 copy-done
  1.7 1.0 copy-done.2
  2.7 1.0 copy-done.4
  3.8 0.7 copy-done.5
  4.5 0.7 copy-done.8
  5.2 0.7 copy-done.10
  5.9 0.7 copy-done.12
  6.6 0.7 copy-done.15
  7.2 1.3 %shard_map.113 = f32[2560,128]{1,0:T(8,128)S(1)} custom-call(f32[2,512,128]{2,1,0:T(8,128)S(1)} %bitcast.21, f32[2,512,128]{2,1,0:T(8,128)S(1)} %bitcast.17, f32[2,512,128]{2,1,0:T(8,128)S(1)} %bitcast.19, f32[2,32]{1,0:T(2,128)S(1)} %copy-done.15, f32[32,32]{1,0:T(8,128)S(1)} %copy-done.5, f32[16,16]{1,0:T(8,128)S(1)} %copy-done.8, ...), custom_call_target="tpu_custom_call" | custom-call | tf_op jit(solution)/shard_map/pallas_call | solution.py:222
  8.5 0.0 copy-start.7
  8.5 0.0 copy-start.14
  8.5 60.4 %all_to_all.10 = f32[512,5,1,128]{3,2,1,0:T(1,128)S(1)} all-to-all(f32[512,5,1,128]{3,2,1,0:T(1,128)S(1)} %bitcast.14), channel_id=1, replica_groups=mesh['wide'=32,'narrow'=16] {'narrow','wide'}, dimensions={0} | all-to-all | bytes 2621440 | tf_op jit(solution)/shard_map/all_to_all | solution.py:228
  69.0 5.3 %shard_map.114 = f32[2048,128]{1,0:T(8,128)S(1)} custom-call(f32[2560,128]{1,0:T(8,128)S(1)} %bitcast.13, f32[64,64]{1,0:T(8,128)S(1)} %copy-done.7, f32[16,16]{1,0:T(8,128)S(1)} %copy-done.14), custom_call_target="tpu_custom_call" | custom-call | tf_op jit(solution)/shard_map/pallas_call | solution.py:232
  74.3 0.0 copy-start.1
  74.3 0.0 copy-start.3
  74.3 0.0 copy-start.6
  74.4 0.0 copy-start.9
  74.4 0.0 copy-start.11
  74.4 0.0 copy-start.13
  74.4 0.0 copy-start.16
  74.4 43.5 %all_to_all.11 = f32[512,4,128]{2,1,0:T(4,128)S(1)} all-to-all(f32[512,4,128]{2,1,0:T(4,128)S(1)} %bitcast.15), channel_id=1, replica_groups=mesh['wide'=32,'narrow'=16] {'narrow','wide'}, dimensions={0} | all-to-all | bytes 2097152 | tf_op jit(solution)/shard_map/all_to_all | solution.py:238
  117.9 0.0 copy-done.1
  117.9 2.1 %shard_map.115 = (f32[2,512,128]{2,1,0:T(8,128)}, f32[2,512,128]{2,1,0:T(8,128)}) custom-call(f32[2048,128]{1,0:T(8,128)S(1)} %bitcast.16, f32[2,512,128]{2,1,0:T(8,128)S(1)} %bitcast.18, f32[2,512,128]{2,1,0:T(8,128)S(1)} %bitcast.20, f32[2,32]{1,0:T(2,128)S(1)} %copy-done.16, f32[32,32]{1,0:T(8,128)S(1)} %copy-done.6, f32[16,16]{1,0:T(8,128)S(1)} %copy-done.9, ...), custom_call_target="tpu_custom_call" | custom-call | tf_op jit(solution)/shard_map/pallas_call | solution.py:241
  (15 shorter events, 0.0 us)
Async XLA Ops:
  0.6 1.0 copy-start
  1.7 1.0 copy-start.2
  2.7 1.0 copy-start.4
  3.8 0.7 copy-start.5
  4.5 0.7 copy-start.8
  5.2 0.7 copy-start.10
  5.9 0.7 copy-start.12
  6.6 0.7 copy-start.15
  8.5 60.5 %copy-start.7 = (f32[64,64]{1,0:T(8,128)S(1)}, f32[64,64]{1,0:T(8,128)}, u32[]{:S(2)}) copy-start(f32[64,64]{1,0:T(8,128)} %refs_1_.1) | copy-start | bytes 49156
  8.5 60.5 %copy-start.14 = (f32[16,16]{1,0:T(8,128)S(1)}, f32[16,16]{1,0:T(8,128)}, u32[]{:S(2)}) copy-start(f32[16,16]{1,0:T(8,128)} %refs_2_.1) | copy-start | bytes 3076
  74.3 43.6 %copy-start.1 = (f32[2,512,1,128]{3,2,1,0:T(1,128)S(1)}, f32[2,512,1,128]{3,2,1,0:T(1,128)}, u32[]{:S(2)}) copy-start(f32[2,512,1,128]{3,2,1,0:T(1,128)} %param.11) | copy-start | bytes 1572868
  74.3 43.5 %copy-start.3 = (f32[2,512,1,128]{3,2,1,0:T(1,128)S(1)}, f32[2,512,1,128]{3,2,1,0:T(1,128)}, u32[]{:S(2)}) copy-start(f32[2,512,1,128]{3,2,1,0:T(1,128)} %param.12) | copy-start | bytes 1572868
  74.3 43.5 %copy-start.6 = (f32[32,32]{1,0:T(8,128)S(1)}, f32[32,32]{1,0:T(8,128)}, u32[]{:S(2)}) copy-start(f32[32,32]{1,0:T(8,128)} %bond_ref.3) | copy-start | bytes 12292
  74.4 43.5 %copy-start.9 = (f32[16,16]{1,0:T(8,128)S(1)}, f32[16,16]{1,0:T(8,128)}, u32[]{:S(2)}) copy-start(f32[16,16]{1,0:T(8,128)} %bend_ref.3) | copy-start | bytes 3076
  74.4 43.5 %copy-start.11 = (f32[16,16]{1,0:T(8,128)S(1)}, f32[16,16]{1,0:T(8,128)}, u32[]{:S(2)}) copy-start(f32[16,16]{1,0:T(8,128)} %torsion_ref.3) | copy-start | bytes 3076
  74.4 43.5 %copy-start.13 = (f32[8,8]{1,0:T(8,128)S(1)}, f32[8,8]{1,0:T(8,128)}, u32[]{:S(2)}) copy-start(f32[8,8]{1,0:T(8,128)} %umbrella_ref.3) | copy-start | bytes 772
  74.4 43.5 %copy-start.16 = (f32[2,32]{1,0:T(2,128)S(1)}, f32[2,32]{1,0:T(2,128)}, u32[]{:S(2)}) copy-start(f32[2,32]{1,0:T(2,128)} %damping_ref.3) | copy-start | bytes 772

commit v2 on v1

v2 whole, which is shorter than its diff:
```python
import jax
import jax.numpy as jnp
from jax import lax
from jax.experimental import pallas as pl
from jax.experimental.pallas import tpu as pltpu
from jax.sharding import PartitionSpec as P

AXES = ("wide", "narrow")
F32 = jnp.float32
BF16 = jnp.bfloat16


def exact_dot(left, right):
    return jnp.dot(left, right, precision=lax.Precision.HIGHEST, preferred_element_type=F32)


def dot(left, right):
    return jnp.dot(left, right, preferred_element_type=F32)


def split(value):
    high = value.astype(BF16)
    return high, (value - high.astype(F32)).astype(BF16)


def iota(shape, axis):
    return lax.broadcasted_iota(jnp.int32, shape, axis)


def ones_where(condition):
    return jnp.where(condition, 1.0, 0.0).astype(F32)


def build_inner(bond_ref, bend_ref, high_ref, low_ref):
    bonds, bends = bond_ref.shape[0], bend_ref.shape[0]
    size = bonds * bends
    spread_bond = exact_dot(bond_ref[...], ones_where(iota((bonds, size), 0) == iota((bonds, size), 1) // bends))
    spread_bend = exact_dot(bend_ref[...], ones_where(iota((bends, size), 0) == iota((bends, size), 1) % bends))
    same_bend = iota((bends, size), 0) == iota((bends, size), 1) % bends
    bond_of = iota((bends, size), 1) // bends
    for bond in range(bonds):
        row = jnp.broadcast_to(spread_bond[bond : bond + 1, :], (bends, size))
        block = jnp.where(same_bend, row, 0.0) + jnp.where(bond_of == bond, spread_bend, 0.0)
        high, low = split(block)
        high_ref[pl.ds(bond * bends, bends), :] = high
        low_ref[pl.ds(bond * bends, bends), :] = low


def build_outer(torsion_ref, umbrella_ref):
    torsions, umbrellas = torsion_ref.shape[0], umbrella_ref.shape[0]
    size = torsions * umbrellas
    spread = ones_where(iota((torsions, size), 0) == iota((torsions, size), 1) // umbrellas)
    spread_rows = ones_where(iota((size, torsions), 1) == iota((size, torsions), 0) // umbrellas)
    tile = ones_where(iota((umbrellas, size), 0) == iota((umbrellas, size), 1) % umbrellas)
    tile_rows = ones_where(iota((size, umbrellas), 1) == iota((size, umbrellas), 0) % umbrellas)
    row, column = iota((size, size), 0), iota((size, size), 1)
    torsion = exact_dot(spread_rows, exact_dot(torsion_ref[...].T, spread))
    umbrella = exact_dot(tile_rows, exact_dot(umbrella_ref[...].T, tile))
    return jnp.where(row % umbrellas == column % umbrellas, torsion, 0.0) + jnp.where(
        row // umbrellas == column // umbrellas, umbrella, 0.0
    )


def damping_columns(damping_ref, size):
    slabs, bonds = damping_ref.shape
    bends = size // bonds
    owner = iota((size, bonds), 0) // bends == iota((size, bonds), 1)
    return [
        jnp.sum(
            jnp.where(owner, jnp.broadcast_to(damping_ref[slab : slab + 1, :], (size, bonds)), 0.0),
            axis=1,
            keepdims=True,
        )
        for slab in range(slabs)
    ]


def outer_parts(torsion_ref, umbrella_ref):
    high, low = split(build_outer(torsion_ref, umbrella_ref))
    return jnp.concatenate([high, high], axis=0), low


def outer_parts(torsion_ref, umbrella_ref):
    high, low = split(build_outer(torsion_ref, umbrella_ref))
    return jnp.concatenate([high, high], axis=0), low


def local_kinetic(fields, high_ref, low_ref, outer_both, outer_low, chunk_rows):
    parts = [split(field) for field in fields]
    high = jnp.concatenate([part[0] for part in parts], axis=1)
    both = jnp.concatenate([high] + [part[1] for part in parts], axis=1)
    width = high.shape[1]
    lanes = fields[0].shape[1]
    for start in range(0, fields[0].shape[0], chunk_rows):
        rows = slice(start, start + chunk_rows)
        product = dot(high_ref[rows], both)
        inner = product[:, :width] + product[:, width:] + dot(low_ref[rows], high)
        yield (
            rows,
            [
                inner[:, at * lanes : (at + 1) * lanes]
                + dot(jnp.concatenate([part_high[rows], part_low[rows]], axis=1), outer_both)
                + dot(part_high[rows], outer_low)
                for at, (part_high, part_low) in enumerate(parts)
            ],
        )


CHUNK = 256


def first_kernel(count, *refs):
    sources, result_ref, targets = refs[:count], refs[count], refs[count + 1 : 2 * count + 1]
    message_ref, high_ref, low_ref, arrived, left = refs[2 * count + 1 :]
    copies = [
        pltpu.make_async_copy(source, target, arrived.at[at])
        for at, (source, target) in enumerate(zip(sources, targets))
    ]
    for copy in copies:
        copy.start()
    bond_ref, bend_ref, torsion_ref, umbrella_ref, damping_ref, curr_ref, potential_ref, prev_ref = targets
    slabs, size, lanes = curr_ref.shape
    stride = 2 * slabs + 1
    for copy in copies[:5]:
        copy.wait()
    build_inner(bond_ref, bend_ref, high_ref, low_ref)
    outer_both, outer_low = outer_parts(torsion_ref, umbrella_ref)
    damping = damping_columns(damping_ref, size)
    factors = jnp.where(iota((size, lanes), 1) < lanes // 2, damping[0], damping[1])
    message_ref[pl.ds(2 * slabs, size, stride=stride), :] = factors
    for copy in copies[5:]:
        copy.wait()
    fields = [curr_ref[slab] for slab in range(slabs)]
    for slab in range(slabs):
        message_ref[pl.ds(slab, size, stride=stride), :] = fields[slab]
    sends = []
    for rows, kinetic in local_kinetic(fields, high_ref, low_ref, outer_both, outer_low, CHUNK):
        for slab in range(slabs):
            total = kinetic[slab] + potential_ref[slab, rows] * fields[slab][rows]
            rest = 2.0 * total - damping[slab][rows] * prev_ref[slab, rows]
            message_ref[pl.ds(rows.start * stride + slabs + slab, CHUNK, stride=stride), :] = rest
        part = pl.ds(rows.start * stride, CHUNK * stride)
        sends.append(pltpu.make_async_copy(message_ref.at[part], result_ref.at[part], left.at[len(sends)]))
        sends[-1].start()
    for send in sends:
        send.wait()


def middle_kernel(slabs, message_ref, radial_ref, twist_ref, back_ref, high_ref, low_ref, along_ref, field_ref):
    lanes = message_ref.shape[1]
    radials, twists = radial_ref.shape[0], twist_ref.shape[0]
    groups = radials // slabs
    size = twists * groups
    stride = 2 * slabs + 1
    block = high_ref.shape[0]

    spread = exact_dot(twist_ref[...], ones_where(iota((twists, block), 0) == iota((twists, block), 1) % twists))
    group_of = iota((twists, block), 1) // twists
    spread_high, spread_low = split(spread)
    zero = jnp.zeros_like(spread_high)
    for at in range(block // twists):
        rows = pl.ds(at * twists, twists)
        high_ref[rows, :] = jnp.where(group_of == at, spread_high, zero)
        low_ref[rows, :] = jnp.where(group_of == at, spread_low, zero)

    square = (radials, radials)
    order = ones_where(iota(square, 0) == (iota(square, 1) % groups) * slabs + iota(square, 1) // groups)
    rows = [radial_ref[pl.ds(slab, groups, stride=slabs), :] for slab in range(slabs)]
    radial_high, radial_low = split(exact_dot(jnp.concatenate(rows, axis=0), order))
    radial = jnp.concatenate([radial_high, radial_high, radial_low, radial_low], axis=1)

    def apply(whole, lines):
        for pair in range(0, twists, 2):
            stacks = []
            for twist in (pair, pair + 1):
                parts = [split(lines(slab, twist)) for slab in range(slabs)]
                stack = [part[0] for part in parts] + [part[1] for part in parts]
                stacks.append(jnp.concatenate(stack + stack, axis=0))
            along = dot(radial, jnp.concatenate(stacks, axis=1))
            for at, twist in enumerate((pair, pair + 1)):
                for slab in range(slabs):
                    along_ref[slab, pl.ds(twist, groups, stride=twists), :] = along[
                        slab * groups : (slab + 1) * groups, at * lanes : (at + 1) * lanes
                    ]
        for start in range(0, size, block):
            rows = slice(start, start + block)
            parts = [split(whole(slab)[rows]) for slab in range(slabs)]
            high = jnp.concatenate([part[0] for part in parts], axis=1)
            both = jnp.concatenate([high] + [part[1] for part in parts], axis=1)
            width = high.shape[1]
            product = dot(high_ref[...], both)
            across = product[:, :width] + product[:, width:] + dot(low_ref[...], high)
            yield rows, [along_ref[slab, rows] + across[:, slab * lanes : (slab + 1) * lanes] for slab in range(slabs)]

    def packet(slab):
        return message_ref[pl.ds(slab, size, stride=stride), :]

    def packet_lines(slab, twist):
        return message_ref[pl.ds(twist * stride + slab, groups, stride=twists * stride), :]

    for rows, turned in apply(packet, packet_lines):
        factors = message_ref[pl.ds(rows.start * stride + 2 * slabs, block, stride=stride), :]
        for slab in range(slabs):
            rest = message_ref[pl.ds(rows.start * stride + slabs + slab, block, stride=stride), :]
            place = slab * (lanes // 2)
            following = factors[:, place : place + 1] * (rest + 2.0 * turned[slab])
            field_ref[slab, rows] = following
            back_ref[pl.ds(rows.start * 2 * slabs + slab, block, stride=2 * slabs), :] = following

    def field(slab):
        return field_ref[slab]

    def field_lines(slab, twist):
        return field_ref[slab, pl.ds(twist, groups, stride=twists), :]

    for rows, turned in apply(field, field_lines):
        for slab in range(slabs):
            back_ref[pl.ds(rows.start * 2 * slabs + slabs + slab, block, stride=2 * slabs), :] = turned[slab]


def last_kernel(
    back_ref,
    curr_ref,
    potential_ref,
    damping_ref,
    bond_ref,
    bend_ref,
    torsion_ref,
    umbrella_ref,
    next_ref,
    last_ref,
    high_ref,
    low_ref,
    next_held,
    last_held,
    left,
):
    slabs, size, _ = curr_ref.shape
    stride = 2 * slabs
    fields = [back_ref[pl.ds(slab, size, stride=stride), :] for slab in range(slabs)]
    for slab in range(slabs):
        next_held[slab] = fields[slab]
    sends = [pltpu.make_async_copy(next_held, next_ref, left.at[0])]
    sends[0].start()
    build_inner(bond_ref, bend_ref, high_ref, low_ref)
    outer_both, outer_low = outer_parts(torsion_ref, umbrella_ref)
    damping = damping_columns(damping_ref, size)
    for rows, kinetic in local_kinetic(fields, high_ref, low_ref, outer_both, outer_low, CHUNK):
        for slab in range(slabs):
            remote = back_ref[pl.ds(rows.start * stride + slabs + slab, CHUNK, stride=stride), :]
            total = kinetic[slab] + remote + potential_ref[slab, rows] * fields[slab][rows]
            factor = damping[slab][rows]
            last_held[slab, rows] = factor * (2.0 * total - factor * curr_ref[slab, rows])
            part = pl.ds(rows.start, CHUNK)
            sends.append(
                pltpu.make_async_copy(last_held.at[slab, part], last_ref.at[slab, part], left.at[len(sends)])
            )
            sends[-1].start()
    for send in sends:
        send.wait()


def params(mebibytes):
    return pltpu.CompilerParams(vmem_limit_bytes=mebibytes * 1024 * 1024)


def shaped(*shape, dtype=F32):
    return jax.ShapeDtypeStruct(shape, dtype)


def local(
    packet_prev,
    packet_curr,
    potential,
    damping,
    kinetic_radial,
    kinetic_bond,
    kinetic_bend,
    kinetic_twist,
    kinetic_torsion,
    kinetic_umbrella,
):
    slabs, size, _, lanes = packet_curr.shape
    flat = (slabs, size, lanes)
    inner = (kinetic_bond, kinetic_bend, kinetic_torsion, kinetic_umbrella)
    prev, curr, field = (value.reshape(flat) for value in (packet_prev, packet_curr, potential))
    stride = 2 * slabs + 1
    sources = (*inner, damping, curr, field, prev)
    whole = pl.BlockSpec(memory_space=pltpu.VMEM)
    remote = pl.BlockSpec(memory_space=pltpu.HBM)
    chunks = size // CHUNK
    matrix = [pltpu.VMEM((size, size), BF16)] * 2
    message = pl.pallas_call(
        lambda *refs: first_kernel(len(sources), *refs),
        out_shape=shaped(size * stride, lanes),
        in_specs=[remote] * len(sources),
        out_specs=remote,
        scratch_shapes=[pltpu.VMEM(source.shape, F32) for source in sources]
        + [pltpu.VMEM((size * stride, lanes), F32)]
        + matrix
        + [pltpu.SemaphoreType.DMA((len(sources),)), pltpu.SemaphoreType.DMA((chunks,))],
        compiler_params=params(60),
    )(*sources)
    message = lax.all_to_all(
        message.reshape(size, stride, 1, lanes), AXES, split_axis=0, concat_axis=0, tiled=True
    ).reshape(size * stride, lanes)
    rows = kinetic_twist.shape[0] * (kinetic_radial.shape[0] // slabs)
    block = 256
    back = pl.pallas_call(
        lambda *refs: middle_kernel(slabs, *refs),
        out_shape=shaped(rows * 2 * slabs, lanes),
        scratch_shapes=[pltpu.VMEM((block, block), BF16)] * 2 + [pltpu.VMEM((slabs, rows, lanes), F32)] * 2,
        compiler_params=params(32),
    )(message, kinetic_radial, kinetic_twist)
    back = lax.all_to_all(
        back.reshape(size, 2 * slabs, lanes), AXES, split_axis=0, concat_axis=0, tiled=True
    ).reshape(size * 2 * slabs, lanes)
    next_term, last_term = pl.pallas_call(
        last_kernel,
        out_shape=(shaped(*flat), shaped(*flat)),
        in_specs=[whole] * 8,
        out_specs=(remote, remote),
        scratch_shapes=matrix
        + [pltpu.VMEM(flat, F32)] * 2
        + [pltpu.SemaphoreType.DMA((1 + slabs * chunks,))],
        compiler_params=params(32),
    )(back, curr, field, damping, *inner)
    return next_term.reshape(packet_curr.shape), last_term.reshape(packet_curr.shape)


def solution(mesh):
    placed = (
        P("wide", None, "narrow", None),
        P("wide", None, "narrow", None),
        P("wide", None, "narrow", None),
        P("wide", None),
        P(),
        P(),
        P(),
        P(),
        P(),
        P(),
    )
    return jax.shard_map(
        local,
        mesh=mesh,
        in_specs=placed,
        out_specs=(P("wide", None, "narrow", None), P("wide", None, "narrow", None)),
        check_vma=False,
    )
```

time: 121 us -> 111 us (0.917)
  local copies, waits for them, and re-layouts: 6.65 us -> 0.06 us
  Pallas kernels: 8.69 us -> 6.93 us
    unnamed x34 -> x18, local copies, waits for them, and re-layouts: 6.65 us -> 0.06 us
    all_to_all x1, blocking collectives: 43.5 us -> 41.5 us  [local(): lax.all_to_all(back.reshape(size, 2 * slabs, lanes), AXES, split_axis=0,...]
    pallas_call x3, Pallas kernels: 8.69 us -> 6.93 us  [the longest x1 3.22 us: local(): pl.pallas_call(lambda *refs: first_kernel(len(sources), *refs), out_shape...]
    all_to_all x1, blocking collectives: 60.4 us -> 61.9 us  [local(): lax.all_to_all(message.reshape(size, stride, 1, lanes), AXES, split_axis=...]
where the time goes in v2:
time: 111 us
  blocking collectives  103 us (93%)
  Pallas kernels  6.93 us (6%)
    all_to_all x1, blocking collectives, local(): lax.all_to_all(message.reshape(size, stride, 1, lanes), AXES, split_axis=...  61.9 us
    all_to_all x1, blocking collectives, local(): lax.all_to_all(back.reshape(size, 2 * slabs, lanes), AXES, split_axis=0,...  41.5 us
    pallas_call x1, Pallas kernels, local(): pl.pallas_call(lambda *refs: first_kernel(len(sources), *refs), out_shape...  3.22 us

profile of v2, /device:TPU:1, one launch (start us, length us, event | category | flops | bytes accessed | tf_op | source)
XLA Modules:
  0.0 111.1 jit_solution(10067366163792445346)
XLA Ops:
  0.6 3.2 %shard_map.113 = f32[2560,128]{1,0:T(8,128)} custom-call(f32[32,32]{1,0:T(8,128)} %bond_ref.1, f32[16,16]{1,0:T(8,128)} %bend_ref.1, f32[16,16]{1,0:T(8,128)} %torsion_ref.1, f32[8,8]{1,0:T(8,128)} %umbrella_ref.1, f32[2,32]{1,0:T(2,128)} %damping_ref.1, f32[2,512,128]{2,1,0:T(8,128)} %bitcast.16, f32[2,512,128]{2,1,0:T(8,128)} %bitcast.18, ...), custom_call_target="tpu_custom_call" | custom-call | tf_op jit(solution)/shard_map/pallas_call | solution.py:293
  3.9 0.0 copy-start.3
  3.9 0.0 copy-start.7
  3.9 61.9 %all_to_all.10 = f32[512,5,1,128]{3,2,1,0:T(1,128)S(1)} all-to-all(f32[512,5,1,128]{3,2,1,0:T(1,128)} %bitcast.20), channel_id=1, replica_groups=mesh['wide'=32,'narrow'=16] {'wide','narrow'}, dimensions={0} | all-to-all | bytes 2621440 | tf_op jit(solution)/shard_map/all_to_all | solution.py:304
  65.8 0.0 copy-done.3
  65.8 0.0 copy-done.7
  65.8 1.6 %shard_map.114 = f32[2048,128]{1,0:T(8,128)S(1)} custom-call(f32[2560,128]{1,0:T(8,128)S(1)} %bitcast.13, f32[64,64]{1,0:T(8,128)S(1)} %copy-done.3, f32[16,16]{1,0:T(8,128)S(1)} %copy-done.7), custom_call_target="tpu_custom_call" | custom-call | tf_op jit(solution)/shard_map/pallas_call | solution.py:309
  67.4 0.0 copy-start
  67.4 0.0 copy-start.1
  67.4 0.0 copy-start.2
  67.4 0.0 copy-start.4
  67.4 0.0 copy-start.5
  67.4 0.0 copy-start.6
  67.4 0.0 copy-start.8
  67.4 41.5 %all_to_all.11 = f32[512,4,128]{2,1,0:T(4,128)S(1)} all-to-all(f32[512,4,128]{2,1,0:T(4,128)S(1)} %bitcast.14), channel_id=1, replica_groups=mesh['wide'=32,'narrow'=16] {'wide','narrow'}, dimensions={0} | all-to-all | bytes 2097152 | tf_op jit(solution)/shard_map/all_to_all | solution.py:315
  108.9 0.0 copy-done
  108.9 0.0 copy-done.1
  108.9 0.0 copy-done.2
  108.9 0.0 copy-done.4
  108.9 0.0 copy-done.5
  109.0 0.0 copy-done.6
  109.0 0.0 copy-done.8
  109.0 2.1 %shard_map.115 = (f32[2,512,128]{2,1,0:T(8,128)}, f32[2,512,128]{2,1,0:T(8,128)}) custom-call(f32[2048,128]{1,0:T(8,128)S(1)} %bitcast.15, f32[2,512,128]{2,1,0:T(8,128)S(1)} %bitcast.17, f32[2,512,128]{2,1,0:T(8,128)S(1)} %bitcast.19, f32[2,32]{1,0:T(2,128)S(1)} %copy-done.8, f32[32,32]{1,0:T(8,128)S(1)} %copy-done.2, f32[16,16]{1,0:T(8,128)S(1)} %copy-done.4, ...), custom_call_target="tpu_custom_call" | custom-call | tf_op jit(solution)/shard_map/pallas_call | solution.py:318
Async XLA Ops:
  3.9 61.9 %copy-start.3 = (f32[64,64]{1,0:T(8,128)S(1)}, f32[64,64]{1,0:T(8,128)}, u32[]{:S(2)}) copy-start(f32[64,64]{1,0:T(8,128)} %refs_1_.3) | copy-start | bytes 49156
  3.9 61.9 %copy-start.7 = (f32[16,16]{1,0:T(8,128)S(1)}, f32[16,16]{1,0:T(8,128)}, u32[]{:S(2)}) copy-start(f32[16,16]{1,0:T(8,128)} %refs_2_.3) | copy-start | bytes 3076
  67.4 41.6 %copy-start = (f32[2,512,1,128]{3,2,1,0:T(1,128)S(1)}, f32[2,512,1,128]{3,2,1,0:T(1,128)}, u32[]{:S(2)}) copy-start(f32[2,512,1,128]{3,2,1,0:T(1,128)} %param.11) | copy-start | bytes 1572868
  67.4 41.6 %copy-start.1 = (f32[2,512,1,128]{3,2,1,0:T(1,128)S(1)}, f32[2,512,1,128]{3,2,1,0:T(1,128)}, u32[]{:S(2)}) copy-start(f32[2,512,1,128]{3,2,1,0:T(1,128)} %param.12) | copy-start | bytes 1572868
  67.4 41.6 %copy-start.2 = (f32[32,32]{1,0:T(8,128)S(1)}, f32[32,32]{1,0:T(8,128)}, u32[]{:S(2)}) copy-start(f32[32,32]{1,0:T(8,128)} %bond_ref.1) | copy-start | bytes 12292
  67.4 41.5 %copy-start.4 = (f32[16,16]{1,0:T(8,128)S(1)}, f32[16,16]{1,0:T(8,128)}, u32[]{:S(2)}) copy-start(f32[16,16]{1,0:T(8,128)} %bend_ref.1) | copy-start | bytes 3076
  67.4 41.5 %copy-start.5 = (f32[16,16]{1,0:T(8,128)S(1)}, f32[16,16]{1,0:T(8,128)}, u32[]{:S(2)}) copy-start(f32[16,16]{1,0:T(8,128)} %torsion_ref.1) | copy-start | bytes 3076
  67.4 41.5 %copy-start.6 = (f32[8,8]{1,0:T(8,128)S(1)}, f32[8,8]{1,0:T(8,128)}, u32[]{:S(2)}) copy-start(f32[8,8]{1,0:T(8,128)} %umbrella_ref.1) | copy-start | bytes 772
  67.4 41.5 %copy-start.8 = (f32[2,32]{1,0:T(2,128)S(1)}, f32[2,32]{1,0:T(2,128)}, u32[]{:S(2)}) copy-start(f32[2,32]{1,0:T(2,128)} %damping_ref.1) | copy-start | bytes 772

commit v3 on v2

--- a/solution.py
+++ b/solution.py
@@ -46,19 +46,23 @@
         low_ref[pl.ds(bond * bends, bends), :] = low
 
 
-def build_outer(torsion_ref, umbrella_ref):
+def build_outer(torsion_ref, umbrella_ref, both_ref, low_ref):
     torsions, umbrellas = torsion_ref.shape[0], umbrella_ref.shape[0]
     size = torsions * umbrellas
-    spread = ones_where(iota((torsions, size), 0) == iota((torsions, size), 1) // umbrellas)
-    spread_rows = ones_where(iota((size, torsions), 1) == iota((size, torsions), 0) // umbrellas)
-    tile = ones_where(iota((umbrellas, size), 0) == iota((umbrellas, size), 1) % umbrellas)
-    tile_rows = ones_where(iota((size, umbrellas), 1) == iota((size, umbrellas), 0) % umbrellas)
-    row, column = iota((size, size), 0), iota((size, size), 1)
-    torsion = exact_dot(spread_rows, exact_dot(torsion_ref[...].T, spread))
-    umbrella = exact_dot(tile_rows, exact_dot(umbrella_ref[...].T, tile))
-    return jnp.where(row % umbrellas == column % umbrellas, torsion, 0.0) + jnp.where(
-        row // umbrellas == column // umbrellas, umbrella, 0.0
-    )
+    place = iota((umbrellas, size), 0)
+    column = iota((umbrellas, size), 1)
+    spread = exact_dot(torsion_ref[...], ones_where(iota((torsions, size), 0) == iota((torsions, size), 1) // umbrellas))
+    tile = exact_dot(umbrella_ref[...], ones_where(place == column % umbrellas))
+    blocks = []
+    for torsion in range(torsions):
+        row = jnp.broadcast_to(spread[torsion : torsion + 1, :], (umbrellas, size))
+        blocks.append(
+            jnp.where(place == column % umbrellas, row, 0.0) + jnp.where(column // umbrellas == torsion, tile, 0.0)
+        )
+    high, low = split(jnp.concatenate(blocks, axis=0))
+    both_ref[pl.ds(0, size), :] = high
+    both_ref[pl.ds(size, size), :] = high
+    low_ref[...] = low
 
 
 def damping_columns(damping_ref, size):
@@ -75,17 +79,7 @@
     ]
 
 
-def outer_parts(torsion_ref, umbrella_ref):
-    high, low = split(build_outer(torsion_ref, umbrella_ref))
-    return jnp.concatenate([high, high], axis=0), low
-
-
-def outer_parts(torsion_ref, umbrella_ref):
-    high, low = split(build_outer(torsion_ref, umbrella_ref))
-    return jnp.concatenate([high, high], axis=0), low
-
-
-def local_kinetic(fields, high_ref, low_ref, outer_both, outer_low, chunk_rows):
+def local_kinetic(fields, high_ref, low_ref, both_ref, rest_ref, chunk_rows):
     parts = [split(field) for field in fields]
     high = jnp.concatenate([part[0] for part in parts], axis=1)
     both = jnp.concatenate([high] + [part[1] for part in parts], axis=1)
@@ -99,19 +93,20 @@
             rows,
             [
                 inner[:, at * lanes : (at + 1) * lanes]
-                + dot(jnp.concatenate([part_high[rows], part_low[rows]], axis=1), outer_both)
-                + dot(part_high[rows], outer_low)
+                + dot(jnp.concatenate([part_high[rows], part_low[rows]], axis=1), both_ref[...])
+                + dot(part_high[rows], rest_ref[...])
                 for at, (part_high, part_low) in enumerate(parts)
             ],
         )
 
 
-CHUNK = 256
+CHUNK = 512
 
 
 def first_kernel(count, *refs):
-    sources, result_ref, targets = refs[:count], refs[count], refs[count + 1 : 2 * count + 1]
-    message_ref, high_ref, low_ref, arrived, left = refs[2 * count + 1 :]
+    sources, results, targets = refs[:count], refs[count : count + 5], refs[count + 5 : 2 * count + 5]
+    message_ref, *matrices = results
+    arrived = refs[2 * count + 5]
     copies = [
         pltpu.make_async_copy(source, target, arrived.at[at])
         for at, (source, target) in enumerate(zip(sources, targets))
@@ -123,27 +118,23 @@
     stride = 2 * slabs + 1
     for copy in copies[:5]:
         copy.wait()
-    build_inner(bond_ref, bend_ref, high_ref, low_ref)
-    outer_both, outer_low = outer_parts(torsion_ref, umbrella_ref)
+    build_outer(torsion_ref, umbrella_ref, *matrices[2:])
+    build_inner(bond_ref, bend_ref, *matrices[:2])
     damping = damping_columns(damping_ref, size)
     factors = jnp.where(iota((size, lanes), 1) < lanes // 2, damping[0], damping[1])
     message_ref[pl.ds(2 * slabs, size, stride=stride), :] = factors
-    for copy in copies[5:]:
-        copy.wait()
+    copies[5].wait()
     fields = [curr_ref[slab] for slab in range(slabs)]
     for slab in range(slabs):
         message_ref[pl.ds(slab, size, stride=stride), :] = fields[slab]
-    sends = []
-    for rows, kinetic in local_kinetic(fields, high_ref, low_ref, outer_both, outer_low, CHUNK):
+    for rows, kinetic in local_kinetic(fields, *matrices, CHUNK):
+        if rows.start == 0:
+            copies[6].wait()
+            copies[7].wait()
         for slab in range(slabs):
             total = kinetic[slab] + potential_ref[slab, rows] * fields[slab][rows]
             rest = 2.0 * total - damping[slab][rows] * prev_ref[slab, rows]
             message_ref[pl.ds(rows.start * stride + slabs + slab, CHUNK, stride=stride), :] = rest
-        part = pl.ds(rows.start * stride, CHUNK * stride)
-        sends.append(pltpu.make_async_copy(message_ref.at[part], result_ref.at[part], left.at[len(sends)]))
-        sends[-1].start()
-    for send in sends:
-        send.wait()
 
 
 def middle_kernel(slabs, message_ref, radial_ref, twist_ref, back_ref, high_ref, low_ref, along_ref, field_ref):
@@ -167,15 +158,15 @@
     order = ones_where(iota(square, 0) == (iota(square, 1) % groups) * slabs + iota(square, 1) // groups)
     rows = [radial_ref[pl.ds(slab, groups, stride=slabs), :] for slab in range(slabs)]
     radial_high, radial_low = split(exact_dot(jnp.concatenate(rows, axis=0), order))
-    radial = jnp.concatenate([radial_high, radial_high, radial_low, radial_low], axis=1)
+    radial = jnp.concatenate([radial_high, radial_high, radial_low], axis=1)
 
     def apply(whole, lines):
         for pair in range(0, twists, 2):
             stacks = []
             for twist in (pair, pair + 1):
                 parts = [split(lines(slab, twist)) for slab in range(slabs)]
-                stack = [part[0] for part in parts] + [part[1] for part in parts]
-                stacks.append(jnp.concatenate(stack + stack, axis=0))
+                high = [part[0] for part in parts]
+                stacks.append(jnp.concatenate(high + [part[1] for part in parts] + high, axis=0))
             along = dot(radial, jnp.concatenate(stacks, axis=1))
             for at, twist in enumerate((pair, pair + 1)):
                 for slab in range(slabs):
@@ -219,21 +210,7 @@
 
 
 def last_kernel(
-    back_ref,
-    curr_ref,
-    potential_ref,
-    damping_ref,
-    bond_ref,
-    bend_ref,
-    torsion_ref,
-    umbrella_ref,
-    next_ref,
-    last_ref,
-    high_ref,
-    low_ref,
-    next_held,
-    last_held,
-    left,
+    back_ref, curr_ref, potential_ref, damping_ref, high_ref, low_ref, both_ref, rest_ref, next_ref, last_ref, next_held, last_held, left
 ):
     slabs, size, _ = curr_ref.shape
     stride = 2 * slabs
@@ -242,10 +219,8 @@
         next_held[slab] = fields[slab]
     sends = [pltpu.make_async_copy(next_held, next_ref, left.at[0])]
     sends[0].start()
-    build_inner(bond_ref, bend_ref, high_ref, low_ref)
-    outer_both, outer_low = outer_parts(torsion_ref, umbrella_ref)
     damping = damping_columns(damping_ref, size)
-    for rows, kinetic in local_kinetic(fields, high_ref, low_ref, outer_both, outer_low, CHUNK):
+    for rows, kinetic in local_kinetic(fields, high_ref, low_ref, both_ref, rest_ref, CHUNK):
         for slab in range(slabs):
             remote = back_ref[pl.ds(rows.start * stride + slabs + slab, CHUNK, stride=stride), :]
             total = kinetic[slab] + remote + potential_ref[slab, rows] * fields[slab][rows]
@@ -285,21 +260,26 @@
     inner = (kinetic_bond, kinetic_bend, kinetic_torsion, kinetic_umbrella)
     prev, curr, field = (value.reshape(flat) for value in (packet_prev, packet_curr, potential))
     stride = 2 * slabs + 1
-    sources = (*inner, damping, curr, field, prev)
+    sources = tuple(
+        pltpu.with_memory_space_constraint(value, pltpu.HBM) for value in (*inner, damping, curr, field, prev)
+    )
     whole = pl.BlockSpec(memory_space=pltpu.VMEM)
     remote = pl.BlockSpec(memory_space=pltpu.HBM)
     chunks = size // CHUNK
-    matrix = [pltpu.VMEM((size, size), BF16)] * 2
-    message = pl.pallas_call(
+    message, *matrices = pl.pallas_call(
         lambda *refs: first_kernel(len(sources), *refs),
-        out_shape=shaped(size * stride, lanes),
+        out_shape=(
+            shaped(size * stride, lanes),
+            shaped(size, size, dtype=BF16),
+            shaped(size, size, dtype=BF16),
+            shaped(2 * lanes, lanes, dtype=BF16),
+            shaped(lanes, lanes, dtype=BF16),
+        ),
         in_specs=[remote] * len(sources),
-        out_specs=remote,
+        out_specs=[whole] * 5,
         scratch_shapes=[pltpu.VMEM(source.shape, F32) for source in sources]
-        + [pltpu.VMEM((size * stride, lanes), F32)]
-        + matrix
-        + [pltpu.SemaphoreType.DMA((len(sources),)), pltpu.SemaphoreType.DMA((chunks,))],
-        compiler_params=params(60),
+        + [pltpu.SemaphoreType.DMA((len(sources),))],
+        compiler_params=params(32),
     )(*sources)
     message = lax.all_to_all(
         message.reshape(size, stride, 1, lanes), AXES, split_axis=0, concat_axis=0, tiled=True
@@ -320,11 +300,9 @@
         out_shape=(shaped(*flat), shaped(*flat)),
         in_specs=[whole] * 8,
         out_specs=(remote, remote),
-        scratch_shapes=matrix
-        + [pltpu.VMEM(flat, F32)] * 2
-        + [pltpu.SemaphoreType.DMA((1 + slabs * chunks,))],
+        scratch_shapes=[pltpu.VMEM(flat, F32)] * 2 + [pltpu.SemaphoreType.DMA((1 + slabs * chunks,))],
         compiler_params=params(32),
-    )(back, curr, field, damping, *inner)
+    )(back, curr, field, damping, *matrices)
     return next_term.reshape(packet_curr.shape), last_term.reshape(packet_curr.shape)
 
 

time: 111 us -> 110 us (level)
  Pallas kernels: 6.93 us -> 5.57 us
where the time goes in v3:
time: 110 us; the launch traced here: 109 us
  blocking collectives  103 us (94%)
  Pallas kernels  5.57 us (5%)
    all_to_all x1, blocking collectives, local(): lax.all_to_all(message.reshape(size, stride, 1, lanes), AXES, split_axis=...  61.6 us
    all_to_all x1, blocking collectives, local(): lax.all_to_all(back.reshape(size, 2 * slabs, lanes), AXES, split_axis=0,...  41.5 us
    pallas_call x1, Pallas kernels, local(): pl.pallas_call(lambda *refs: first_kernel(len(sources), *refs), out_shape...  2.24 us

profile of v3, /device:TPU:1, one launch (start us, length us, event | category | flops | bytes accessed | tf_op | source)
XLA Modules:
  0.0 109.4 jit_solution(2245183384853552983)
XLA Ops:
  0.6 2.2 %shard_map.113 = (f32[2560,128]{1,0:T(8,128)S(1)}, bf16[512,512]{1,0:T(8,128)(2,1)S(1)}, bf16[512,512]{1,0:T(8,128)(2,1)S(1)}, bf16[256,128]{1,0:T(8,128)(2,1)S(1)}, bf16[128,128]{1,0:T(8,128)(2,1)S(1)}) custom-call(f32[32,32]{1,0:T(8,128)} %refs_0_.1, f32[16,16]{1,0:T(8,128)} %refs_1_.2, f32[16,16]{1,0:T(8,128)} %refs_2_.2, f32[8,8]{1,0:T(8,128)} %refs_3_.1, ...), custom_call_target="tpu_custom_call" | custom-call | tf_op jit(solution)/shard_map/pallas_call | solution.py:269
  2.9 0.0 copy-start.2
  2.9 0.0 copy-start.3
  2.9 61.6 %all_to_all.10 = f32[512,5,1,128]{3,2,1,0:T(1,128)S(1)} all-to-all(f32[512,5,1,128]{3,2,1,0:T(1,128)S(1)} %bitcast.20), channel_id=1, replica_groups=mesh['wide'=32,'narrow'=16] {'wide','narrow'}, dimensions={0} | all-to-all | bytes 2621440 | tf_op jit(solution)/shard_map/all_to_all | solution.py:284
  64.6 0.0 copy-done.2
  64.6 0.0 copy-done.3
  64.6 1.5 %shard_map.114 = f32[2048,128]{1,0:T(8,128)S(1)} custom-call(f32[2560,128]{1,0:T(8,128)S(1)} %bitcast.13, f32[64,64]{1,0:T(8,128)S(1)} %copy-done.2, f32[16,16]{1,0:T(8,128)S(1)} %copy-done.3), custom_call_target="tpu_custom_call" | custom-call | tf_op jit(solution)/shard_map/pallas_call | solution.py:289
  66.1 0.0 copy-start
  66.1 0.0 copy-start.1
  66.1 0.0 copy-start.4
  66.1 41.5 %all_to_all.11 = f32[512,4,128]{2,1,0:T(4,128)S(1)} all-to-all(f32[512,4,128]{2,1,0:T(4,128)S(1)} %bitcast.14), channel_id=1, replica_groups=mesh['wide'=32,'narrow'=16] {'wide','narrow'}, dimensions={0} | all-to-all | bytes 2097152 | tf_op jit(solution)/shard_map/all_to_all | solution.py:295
  107.6 0.0 copy-done
  107.6 0.0 copy-done.1
  107.6 0.0 copy-done.4
  107.6 1.8 %shard_map.115 = (f32[2,512,128]{2,1,0:T(8,128)}, f32[2,512,128]{2,1,0:T(8,128)}) custom-call(f32[2048,128]{1,0:T(8,128)S(1)} %bitcast.15, f32[2,512,128]{2,1,0:T(8,128)S(1)} %bitcast.17, f32[2,512,128]{2,1,0:T(8,128)S(1)} %bitcast.19, f32[2,32]{1,0:T(2,128)S(1)} %copy-done.4, bf16[512,512]{1,0:T(8,128)(2,1)S(1)} %get-tuple-element.10.high_ref, ...), custom_call_target="tpu_custom_call" | custom-call | tf_op jit(solution)/shard_map/pallas_call | solution.py:298
Async XLA Ops:
  2.9 61.7 %copy-start.2 = (f32[64,64]{1,0:T(8,128)S(1)}, f32[64,64]{1,0:T(8,128)}, u32[]{:S(2)}) copy-start(f32[64,64]{1,0:T(8,128)} %refs_1_.3) | copy-start | bytes 49156
  2.9 61.7 %copy-start.3 = (f32[16,16]{1,0:T(8,128)S(1)}, f32[16,16]{1,0:T(8,128)}, u32[]{:S(2)}) copy-start(f32[16,16]{1,0:T(8,128)} %refs_2_.3) | copy-start | bytes 3076
  66.1 41.5 %copy-start = (f32[2,512,1,128]{3,2,1,0:T(1,128)S(1)}, f32[2,512,1,128]{3,2,1,0:T(1,128)}, u32[]{:S(2)}) copy-start(f32[2,512,1,128]{3,2,1,0:T(1,128)} %param.11) | copy-start | bytes 1572868
  66.1 41.5 %copy-start.1 = (f32[2,512,1,128]{3,2,1,0:T(1,128)S(1)}, f32[2,512,1,128]{3,2,1,0:T(1,128)}, u32[]{:S(2)}) copy-start(f32[2,512,1,128]{3,2,1,0:T(1,128)} %param.12) | copy-start | bytes 1572868
  66.1 41.5 %copy-start.4 = (f32[2,32]{1,0:T(2,128)S(1)}, f32[2,32]{1,0:T(2,128)}, u32[]{:S(2)}) copy-start(f32[2,32]{1,0:T(2,128)} %damping_ref.1) | copy-start | bytes 772

commit v4 on v3

--- a/solution.py
+++ b/solution.py
@@ -100,7 +100,7 @@
         )
 
 
-CHUNK = 512
+LAST_CHUNK = 256
 
 
 def first_kernel(count, *refs):
@@ -127,47 +127,61 @@
     fields = [curr_ref[slab] for slab in range(slabs)]
     for slab in range(slabs):
         message_ref[pl.ds(slab, size, stride=stride), :] = fields[slab]
-    for rows, kinetic in local_kinetic(fields, *matrices, CHUNK):
+    for rows, kinetic in local_kinetic(fields, *matrices, size):
         if rows.start == 0:
             copies[6].wait()
             copies[7].wait()
         for slab in range(slabs):
             total = kinetic[slab] + potential_ref[slab, rows] * fields[slab][rows]
             rest = 2.0 * total - damping[slab][rows] * prev_ref[slab, rows]
-            message_ref[pl.ds(rows.start * stride + slabs + slab, CHUNK, stride=stride), :] = rest
-
-
-def middle_kernel(slabs, message_ref, radial_ref, twist_ref, back_ref, high_ref, low_ref, along_ref, field_ref):
+            message_ref[pl.ds(slabs + slab, size, stride=stride), :] = rest
+
+
+CORES = 2
+
+
+def return_order(wide, narrow):
+    return [(chip * CORES + core) * narrow + at for chip in range(wide // CORES) for at in range(narrow) for core in range(CORES)]
+
+
+def return_rows(peer, run, width, first):
+    chip, core = divmod(peer // run, CORES)
+    return pl.ds((chip * CORES * run + core) * width + first, run, stride=CORES * width)
+
+
+def square_of_parts(high, low):
+    return jnp.concatenate([jnp.concatenate([high, high], axis=1), jnp.concatenate([low, low], axis=1)], axis=0)
+
+
+def middle_kernel(slabs, message_ref, radial_ref, twist_ref, back_ref, along_ref, field_ref):
     lanes = message_ref.shape[1]
     radials, twists = radial_ref.shape[0], twist_ref.shape[0]
     groups = radials // slabs
     size = twists * groups
     stride = 2 * slabs + 1
-    block = high_ref.shape[0]
+    block = 128
 
     spread = exact_dot(twist_ref[...], ones_where(iota((twists, block), 0) == iota((twists, block), 1) % twists))
     group_of = iota((twists, block), 1) // twists
-    spread_high, spread_low = split(spread)
-    zero = jnp.zeros_like(spread_high)
-    for at in range(block // twists):
-        rows = pl.ds(at * twists, twists)
-        high_ref[rows, :] = jnp.where(group_of == at, spread_high, zero)
-        low_ref[rows, :] = jnp.where(group_of == at, spread_low, zero)
+    twist_high, twist_low = split(
+        jnp.concatenate([jnp.where(group_of == at, spread, 0.0) for at in range(block // twists)], axis=0)
+    )
+    twist_square = square_of_parts(twist_high, twist_low)
 
     square = (radials, radials)
     order = ones_where(iota(square, 0) == (iota(square, 1) % groups) * slabs + iota(square, 1) // groups)
     rows = [radial_ref[pl.ds(slab, groups, stride=slabs), :] for slab in range(slabs)]
     radial_high, radial_low = split(exact_dot(jnp.concatenate(rows, axis=0), order))
-    radial = jnp.concatenate([radial_high, radial_high, radial_low], axis=1)
+    radial = square_of_parts(radial_high, radial_low)
 
     def apply(whole, lines):
         for pair in range(0, twists, 2):
             stacks = []
             for twist in (pair, pair + 1):
                 parts = [split(lines(slab, twist)) for slab in range(slabs)]
-                high = [part[0] for part in parts]
-                stacks.append(jnp.concatenate(high + [part[1] for part in parts] + high, axis=0))
+                stacks.append(jnp.concatenate([part[0] for part in parts] + [part[1] for part in parts], axis=0))
             along = dot(radial, jnp.concatenate(stacks, axis=1))
+            along = along[:radials] + along[radials:]
             for at, twist in enumerate((pair, pair + 1)):
                 for slab in range(slabs):
                     along_ref[slab, pl.ds(twist, groups, stride=twists), :] = along[
@@ -176,12 +190,14 @@
         for start in range(0, size, block):
             rows = slice(start, start + block)
             parts = [split(whole(slab)[rows]) for slab in range(slabs)]
-            high = jnp.concatenate([part[0] for part in parts], axis=1)
-            both = jnp.concatenate([high] + [part[1] for part in parts], axis=1)
-            width = high.shape[1]
-            product = dot(high_ref[...], both)
-            across = product[:, :width] + product[:, width:] + dot(low_ref[...], high)
+            both = [jnp.concatenate([part[at] for part in parts], axis=1) for at in range(2)]
+            across = dot(twist_square, jnp.concatenate(both, axis=0))
+            across = across[:block] + across[block:]
             yield rows, [along_ref[slab, rows] + across[:, slab * lanes : (slab + 1) * lanes] for slab in range(slabs)]
+
+    def send(value, start, first):
+        for at in range(0, block, twists):
+            back_ref[return_rows(start + at, twists, 2 * slabs, first), :] = value[at : at + twists]
 
     def packet(slab):
         return message_ref[pl.ds(slab, size, stride=stride), :]
@@ -196,7 +212,7 @@
             place = slab * (lanes // 2)
             following = factors[:, place : place + 1] * (rest + 2.0 * turned[slab])
             field_ref[slab, rows] = following
-            back_ref[pl.ds(rows.start * 2 * slabs + slab, block, stride=2 * slabs), :] = following
+            send(following, rows.start, slab)
 
     def field(slab):
         return field_ref[slab]
@@ -206,27 +222,44 @@
 
     for rows, turned in apply(field, field_lines):
         for slab in range(slabs):
-            back_ref[pl.ds(rows.start * 2 * slabs + slabs + slab, block, stride=2 * slabs), :] = turned[slab]
+            send(turned[slab], rows.start, slabs + slab)
 
 
 def last_kernel(
-    back_ref, curr_ref, potential_ref, damping_ref, high_ref, low_ref, both_ref, rest_ref, next_ref, last_ref, next_held, last_held, left
+    run,
+    back_ref,
+    curr_ref,
+    potential_ref,
+    damping_ref,
+    high_ref,
+    low_ref,
+    both_ref,
+    rest_ref,
+    next_ref,
+    last_ref,
+    next_held,
+    last_held,
+    left,
 ):
     slabs, size, _ = curr_ref.shape
-    stride = 2 * slabs
-    fields = [back_ref[pl.ds(slab, size, stride=stride), :] for slab in range(slabs)]
+
+    def received(start, rows, first):
+        pieces = [back_ref[return_rows(peer, run, 2 * slabs, first), :] for peer in range(start, start + rows, run)]
+        return jnp.concatenate(pieces, axis=0)
+
+    fields = [received(0, size, slab) for slab in range(slabs)]
     for slab in range(slabs):
         next_held[slab] = fields[slab]
     sends = [pltpu.make_async_copy(next_held, next_ref, left.at[0])]
     sends[0].start()
     damping = damping_columns(damping_ref, size)
-    for rows, kinetic in local_kinetic(fields, high_ref, low_ref, both_ref, rest_ref, CHUNK):
+    for rows, kinetic in local_kinetic(fields, high_ref, low_ref, both_ref, rest_ref, LAST_CHUNK):
         for slab in range(slabs):
-            remote = back_ref[pl.ds(rows.start * stride + slabs + slab, CHUNK, stride=stride), :]
+            remote = received(rows.start, LAST_CHUNK, slabs + slab)
             total = kinetic[slab] + remote + potential_ref[slab, rows] * fields[slab][rows]
             factor = damping[slab][rows]
             last_held[slab, rows] = factor * (2.0 * total - factor * curr_ref[slab, rows])
-            part = pl.ds(rows.start, CHUNK)
+            part = pl.ds(rows.start, LAST_CHUNK)
             sends.append(
                 pltpu.make_async_copy(last_held.at[slab, part], last_ref.at[slab, part], left.at[len(sends)])
             )
@@ -256,6 +289,7 @@
     kinetic_umbrella,
 ):
     slabs, size, _, lanes = packet_curr.shape
+    narrow = lax.axis_size("narrow")
     flat = (slabs, size, lanes)
     inner = (kinetic_bond, kinetic_bend, kinetic_torsion, kinetic_umbrella)
     prev, curr, field = (value.reshape(flat) for value in (packet_prev, packet_curr, potential))
@@ -265,7 +299,7 @@
     )
     whole = pl.BlockSpec(memory_space=pltpu.VMEM)
     remote = pl.BlockSpec(memory_space=pltpu.HBM)
-    chunks = size // CHUNK
+    chunks = size // LAST_CHUNK
     message, *matrices = pl.pallas_call(
         lambda *refs: first_kernel(len(sources), *refs),
         out_shape=(
@@ -285,18 +319,22 @@
         message.reshape(size, stride, 1, lanes), AXES, split_axis=0, concat_axis=0, tiled=True
     ).reshape(size * stride, lanes)
     rows = kinetic_twist.shape[0] * (kinetic_radial.shape[0] // slabs)
-    block = 256
     back = pl.pallas_call(
         lambda *refs: middle_kernel(slabs, *refs),
         out_shape=shaped(rows * 2 * slabs, lanes),
-        scratch_shapes=[pltpu.VMEM((block, block), BF16)] * 2 + [pltpu.VMEM((slabs, rows, lanes), F32)] * 2,
+        scratch_shapes=[pltpu.VMEM((slabs, rows, lanes), F32)] * 2,
         compiler_params=params(32),
     )(message, kinetic_radial, kinetic_twist)
     back = lax.all_to_all(
-        back.reshape(size, 2 * slabs, lanes), AXES, split_axis=0, concat_axis=0, tiled=True
+        back.reshape(size, 2 * slabs, lanes),
+        AXES,
+        split_axis=0,
+        concat_axis=0,
+        tiled=True,
+        axis_index_groups=[return_order(lax.axis_size("wide"), narrow)],
     ).reshape(size * 2 * slabs, lanes)
     next_term, last_term = pl.pallas_call(
-        last_kernel,
+        lambda *refs: last_kernel(narrow, *refs),
         out_shape=(shaped(*flat), shaped(*flat)),
         in_specs=[whole] * 8,
         out_specs=(remote, remote),

time: 110 us -> 108 us (0.982)
    all_to_all x1, blocking collectives: 41.5 us -> 39.9 us  [local(): lax.all_to_all(back.reshape(size, 2 * slabs, lanes), AXES, split_axis=0,...]
where the time goes in v4:
time: 108 us
  blocking collectives  102 us (94%)
  Pallas kernels  5.32 us (5%)
    all_to_all x1, blocking collectives, local(): lax.all_to_all(message.reshape(size, stride, 1, lanes), AXES, split_axis=...  61.6 us
    all_to_all x1, blocking collectives, local(): lax.all_to_all(back.reshape(size, 2 * slabs, lanes), AXES, split_axis=0,...  39.9 us
    pallas_call x1, Pallas kernels, local(): pl.pallas_call(lambda *refs: first_kernel(len(sources), *refs), out_shape...  2.24 us

profile of v4, /device:TPU:1, one launch (start us, length us, event | category | flops | bytes accessed | tf_op | source)
XLA Modules:
  0.0 107.6 jit_solution(11057209759663105614)
XLA Ops:
  0.6 2.2 %shard_map.113 = (f32[2560,128]{1,0:T(8,128)S(1)}, bf16[512,512]{1,0:T(8,128)(2,1)S(1)}, bf16[512,512]{1,0:T(8,128)(2,1)S(1)}, bf16[256,128]{1,0:T(8,128)(2,1)S(1)}, bf16[128,128]{1,0:T(8,128)(2,1)S(1)}) custom-call(f32[32,32]{1,0:T(8,128)} %refs_0_.1, f32[16,16]{1,0:T(8,128)} %refs_1_.2, f32[16,16]{1,0:T(8,128)} %refs_2_.2, f32[8,8]{1,0:T(8,128)} %refs_3_.2, ...), custom_call_target="tpu_custom_call" | custom-call | tf_op jit(solution)/shard_map/pallas_call | solution.py:303
  2.9 0.0 copy-start.2
  2.9 0.0 copy-start.3
  2.9 61.6 %all_to_all.10 = f32[512,5,1,128]{3,2,1,0:T(1,128)S(1)} all-to-all(f32[512,5,1,128]{3,2,1,0:T(1,128)S(1)} %bitcast.20), channel_id=1, replica_groups=mesh['wide'=32,'narrow'=16] {'wide','narrow'}, dimensions={0} | all-to-all | bytes 2621440 | tf_op jit(solution)/shard_map/all_to_all | solution.py:318
  64.6 0.0 copy-done.2
  64.6 0.0 copy-done.3
  64.6 1.3 %shard_map.114 = f32[2048,128]{1,0:T(8,128)S(1)} custom-call(f32[2560,128]{1,0:T(8,128)S(1)} %bitcast.13, f32[64,64]{1,0:T(8,128)S(1)} %copy-done.2, f32[16,16]{1,0:T(8,128)S(1)} %copy-done.3), custom_call_target="tpu_custom_call" | custom-call | tf_op jit(solution)/shard_map/pallas_call | solution.py:322
  65.9 0.0 copy-start
  65.9 0.0 copy-start.1
  65.9 0.0 copy-start.4
  65.9 39.9 %all_to_all.11 = f32[512,4,128]{2,1,0:T(4,128)S(1)} all-to-all(f32[512,4,128]{2,1,0:T(4,128)S(1)} %bitcast.14), channel_id=1, replica_groups={{0,16,1,17,2,18,3,19,4,20,5,21,6,22,7,23,8,24,9,25,10,26,11,27,12,28,13..., dimensions={0} | all-to-all | bytes 2097152 | tf_op jit(solution)/shard_map/all_to_all | solution.py:328
  105.9 0.0 copy-done
  105.9 0.0 copy-done.1
  105.9 0.0 copy-done.4
  105.9 1.8 %shard_map.115 = (f32[2,512,128]{2,1,0:T(8,128)}, f32[2,512,128]{2,1,0:T(8,128)}) custom-call(f32[2048,128]{1,0:T(8,128)S(1)} %bitcast.15, f32[2,512,128]{2,1,0:T(8,128)S(1)} %bitcast.17, f32[2,512,128]{2,1,0:T(8,128)S(1)} %bitcast.19, f32[2,32]{1,0:T(2,128)S(1)} %copy-done.4, bf16[512,512]{1,0:T(8,128)(2,1)S(1)} %get-tuple-element.10.refs_4_, ...), custom_call_target="tpu_custom_call" | custom-call | tf_op jit(solution)/shard_map/pallas_call | solution.py:336
Async XLA Ops:
  2.9 61.7 %copy-start.2 = (f32[64,64]{1,0:T(8,128)S(1)}, f32[64,64]{1,0:T(8,128)}, u32[]{:S(2)}) copy-start(f32[64,64]{1,0:T(8,128)} %refs_1_.3) | copy-start | bytes 49156
  2.9 61.7 %copy-start.3 = (f32[16,16]{1,0:T(8,128)S(1)}, f32[16,16]{1,0:T(8,128)}, u32[]{:S(2)}) copy-start(f32[16,16]{1,0:T(8,128)} %refs_2_.3) | copy-start | bytes 3076
  65.9 40.0 %copy-start = (f32[2,512,1,128]{3,2,1,0:T(1,128)S(1)}, f32[2,512,1,128]{3,2,1,0:T(1,128)}, u32[]{:S(2)}) copy-start(f32[2,512,1,128]{3,2,1,0:T(1,128)} %param.11) | copy-start | bytes 1572868
  65.9 40.0 %copy-start.1 = (f32[2,512,1,128]{3,2,1,0:T(1,128)S(1)}, f32[2,512,1,128]{3,2,1,0:T(1,128)}, u32[]{:S(2)}) copy-start(f32[2,512,1,128]{3,2,1,0:T(1,128)} %param.12) | copy-start | bytes 1572868
  65.9 40.0 %copy-start.4 = (f32[2,32]{1,0:T(2,128)S(1)}, f32[2,32]{1,0:T(2,128)}, u32[]{:S(2)}) copy-start(f32[2,32]{1,0:T(2,128)} %refs_3_.3) | copy-start | bytes 772

commit v5 on v4

--- a/solution.py
+++ b/solution.py
@@ -31,22 +31,19 @@
     return jnp.where(condition, 1.0, 0.0).astype(F32)
 
 
-def build_inner(bond_ref, bend_ref, high_ref, low_ref):
-    bonds, bends = bond_ref.shape[0], bend_ref.shape[0]
-    size = bonds * bends
-    spread_bond = exact_dot(bond_ref[...], ones_where(iota((bonds, size), 0) == iota((bonds, size), 1) // bends))
-    spread_bend = exact_dot(bend_ref[...], ones_where(iota((bends, size), 0) == iota((bends, size), 1) % bends))
-    same_bend = iota((bends, size), 0) == iota((bends, size), 1) % bends
-    bond_of = iota((bends, size), 1) // bends
-    for bond in range(bonds):
-        row = jnp.broadcast_to(spread_bond[bond : bond + 1, :], (bends, size))
-        block = jnp.where(same_bend, row, 0.0) + jnp.where(bond_of == bond, spread_bend, 0.0)
-        high, low = split(block)
-        high_ref[pl.ds(bond * bends, bends), :] = high
-        low_ref[pl.ds(bond * bends, bends), :] = low
-
-
-def build_outer(torsion_ref, umbrella_ref, both_ref, low_ref):
+def square_of_parts(high, low):
+    return jnp.concatenate([jnp.concatenate([high, high], axis=1), jnp.concatenate([low, low], axis=1)], axis=0)
+
+
+def repeated(matrix_ref, copies):
+    count = matrix_ref.shape[0]
+    size = count * copies
+    spread = exact_dot(matrix_ref[...], ones_where(iota((count, size), 0) == iota((count, size), 1) % count))
+    copy_of = iota((count, size), 1) // count
+    return jnp.concatenate([jnp.where(copy_of == at, spread, 0.0) for at in range(copies)], axis=0)
+
+
+def build_outer(torsion_ref, umbrella_ref):
     torsions, umbrellas = torsion_ref.shape[0], umbrella_ref.shape[0]
     size = torsions * umbrellas
     place = iota((umbrellas, size), 0)
@@ -60,9 +57,20 @@
             jnp.where(place == column % umbrellas, row, 0.0) + jnp.where(column // umbrellas == torsion, tile, 0.0)
         )
     high, low = split(jnp.concatenate(blocks, axis=0))
-    both_ref[pl.ds(0, size), :] = high
-    both_ref[pl.ds(size, size), :] = high
-    low_ref[...] = low
+    both = jnp.concatenate([high, low], axis=1)
+    return jnp.concatenate([both, both], axis=0)
+
+
+BLOCK = 128
+
+
+def build_local(bond_ref, bend_ref, torsion_ref, umbrella_ref):
+    bends = bend_ref.shape[0]
+    return (
+        square_of_parts(*split(bond_ref[...])),
+        square_of_parts(*split(repeated(bend_ref, BLOCK // bends))),
+        build_outer(torsion_ref, umbrella_ref),
+    )
 
 
 def damping_columns(damping_ref, size):
@@ -79,34 +87,38 @@
     ]
 
 
-def local_kinetic(fields, high_ref, low_ref, both_ref, rest_ref, chunk_rows):
-    parts = [split(field) for field in fields]
-    high = jnp.concatenate([part[0] for part in parts], axis=1)
-    both = jnp.concatenate([high] + [part[1] for part in parts], axis=1)
-    width = high.shape[1]
-    lanes = fields[0].shape[1]
-    for start in range(0, fields[0].shape[0], chunk_rows):
-        rows = slice(start, start + chunk_rows)
-        product = dot(high_ref[rows], both)
-        inner = product[:, :width] + product[:, width:] + dot(low_ref[rows], high)
-        yield (
-            rows,
-            [
-                inner[:, at * lanes : (at + 1) * lanes]
-                + dot(jnp.concatenate([part_high[rows], part_low[rows]], axis=1), both_ref[...])
-                + dot(part_high[rows], rest_ref[...])
-                for at, (part_high, part_low) in enumerate(parts)
-            ],
-        )
-
-
-LAST_CHUNK = 256
+def local_kinetic(field_ref, bond_ref, bond_square, bend_square, outer_square):
+    slabs, size, lanes = field_ref.shape
+    bonds = bond_square.shape[0] // 2
+    bends = size // bonds
+    for bend in range(bends):
+        lines = pl.ds(bend, bonds, stride=bends)
+        parts = [split(field_ref[slab, lines, :]) for slab in range(slabs)]
+        both = [jnp.concatenate([part[at] for part in parts], axis=1) for at in range(2)]
+        along = dot(bond_square, jnp.concatenate(both, axis=0))
+        along = along[:bonds] + along[bonds:]
+        for slab in range(slabs):
+            bond_ref[slab, lines, :] = along[:, slab * lanes : (slab + 1) * lanes]
+    for start in range(0, size, BLOCK):
+        rows = slice(start, start + BLOCK)
+        parts = [split(field_ref[slab, rows]) for slab in range(slabs)]
+        both = [jnp.concatenate([part[at] for part in parts], axis=1) for at in range(2)]
+        across = dot(bend_square, jnp.concatenate(both, axis=0))
+        across = across[:BLOCK] + across[BLOCK:]
+        totals = []
+        for slab in range(slabs):
+            turned = dot(jnp.concatenate(parts[slab], axis=1), outer_square)
+            totals.append(
+                bond_ref[slab, rows]
+                + across[:, slab * lanes : (slab + 1) * lanes]
+                + (turned[:, :lanes] + turned[:, lanes:])
+            )
+        yield rows, totals
 
 
 def first_kernel(count, *refs):
-    sources, results, targets = refs[:count], refs[count : count + 5], refs[count + 5 : 2 * count + 5]
-    message_ref, *matrices = results
-    arrived = refs[2 * count + 5]
+    sources, message_ref, targets = refs[:count], refs[count], refs[count + 1 : 2 * count + 1]
+    along_ref, arrived = refs[2 * count + 1 :]
     copies = [
         pltpu.make_async_copy(source, target, arrived.at[at])
         for at, (source, target) in enumerate(zip(sources, targets))
@@ -118,39 +130,46 @@
     stride = 2 * slabs + 1
     for copy in copies[:5]:
         copy.wait()
-    build_outer(torsion_ref, umbrella_ref, *matrices[2:])
-    build_inner(bond_ref, bend_ref, *matrices[:2])
+    matrices = build_local(bond_ref, bend_ref, torsion_ref, umbrella_ref)
     damping = damping_columns(damping_ref, size)
     factors = jnp.where(iota((size, lanes), 1) < lanes // 2, damping[0], damping[1])
     message_ref[pl.ds(2 * slabs, size, stride=stride), :] = factors
     copies[5].wait()
-    fields = [curr_ref[slab] for slab in range(slabs)]
     for slab in range(slabs):
-        message_ref[pl.ds(slab, size, stride=stride), :] = fields[slab]
-    for rows, kinetic in local_kinetic(fields, *matrices, size):
+        message_ref[pl.ds(slab, size, stride=stride), :] = curr_ref[slab]
+    for rows, kinetic in local_kinetic(curr_ref, along_ref, *matrices):
         if rows.start == 0:
             copies[6].wait()
             copies[7].wait()
         for slab in range(slabs):
-            total = kinetic[slab] + potential_ref[slab, rows] * fields[slab][rows]
+            total = kinetic[slab] + potential_ref[slab, rows] * curr_ref[slab, rows]
             rest = 2.0 * total - damping[slab][rows] * prev_ref[slab, rows]
-            message_ref[pl.ds(slabs + slab, size, stride=stride), :] = rest
+            message_ref[pl.ds(rows.start * stride + slabs + slab, BLOCK, stride=stride), :] = rest
 
 
 CORES = 2
+HALVES = 2
+
+
+def place_of(chip, chips):
+    level, half = divmod(chip, HALVES)
+    return (half + 1) * (chips // HALVES) - 1 - level
 
 
 def return_order(wide, narrow):
-    return [(chip * CORES + core) * narrow + at for chip in range(wide // CORES) for at in range(narrow) for core in range(CORES)]
-
-
-def return_rows(peer, run, width, first):
+    chips = wide // CORES
+    return [
+        (chip * CORES + core) * narrow + at
+        for chip in sorted(range(chips), key=lambda chip: place_of(chip, chips))
+        for at in range(narrow)
+        for core in range(CORES)
+    ]
+
+
+def return_rows(peer, run, size, width, first):
     chip, core = divmod(peer // run, CORES)
-    return pl.ds((chip * CORES * run + core) * width + first, run, stride=CORES * width)
-
-
-def square_of_parts(high, low):
-    return jnp.concatenate([jnp.concatenate([high, high], axis=1), jnp.concatenate([low, low], axis=1)], axis=0)
+    place = place_of(chip, size // (CORES * run))
+    return pl.ds((place * CORES * run + core) * width + first, run, stride=CORES * width)
 
 
 def middle_kernel(slabs, message_ref, radial_ref, twist_ref, back_ref, along_ref, field_ref):
@@ -159,14 +178,9 @@
     groups = radials // slabs
     size = twists * groups
     stride = 2 * slabs + 1
-    block = 128
-
-    spread = exact_dot(twist_ref[...], ones_where(iota((twists, block), 0) == iota((twists, block), 1) % twists))
-    group_of = iota((twists, block), 1) // twists
-    twist_high, twist_low = split(
-        jnp.concatenate([jnp.where(group_of == at, spread, 0.0) for at in range(block // twists)], axis=0)
-    )
-    twist_square = square_of_parts(twist_high, twist_low)
+    block = BLOCK
+
+    twist_square = square_of_parts(*split(repeated(twist_ref, BLOCK // twists)))
 
     square = (radials, radials)
     order = ones_where(iota(square, 0) == (iota(square, 1) % groups) * slabs + iota(square, 1) // groups)
@@ -197,7 +211,7 @@
 
     def send(value, start, first):
         for at in range(0, block, twists):
-            back_ref[return_rows(start + at, twists, 2 * slabs, first), :] = value[at : at + twists]
+            back_ref[return_rows(start + at, twists, size, 2 * slabs, first), :] = value[at : at + twists]
 
     def packet(slab):
         return message_ref[pl.ds(slab, size, stride=stride), :]
@@ -231,39 +245,40 @@
     curr_ref,
     potential_ref,
     damping_ref,
-    high_ref,
-    low_ref,
-    both_ref,
-    rest_ref,
+    bond_ref,
+    bend_ref,
+    torsion_ref,
+    umbrella_ref,
     next_ref,
     last_ref,
     next_held,
     last_held,
+    along_ref,
     left,
 ):
     slabs, size, _ = curr_ref.shape
 
     def received(start, rows, first):
-        pieces = [back_ref[return_rows(peer, run, 2 * slabs, first), :] for peer in range(start, start + rows, run)]
-        return jnp.concatenate(pieces, axis=0)
-
-    fields = [received(0, size, slab) for slab in range(slabs)]
+        peers = range(start, start + rows, run)
+        return jnp.concatenate([back_ref[return_rows(peer, run, size, 2 * slabs, first), :] for peer in peers], axis=0)
+
     for slab in range(slabs):
-        next_held[slab] = fields[slab]
+        next_held[slab] = received(0, size, slab)
     sends = [pltpu.make_async_copy(next_held, next_ref, left.at[0])]
     sends[0].start()
     damping = damping_columns(damping_ref, size)
-    for rows, kinetic in local_kinetic(fields, high_ref, low_ref, both_ref, rest_ref, LAST_CHUNK):
-        for slab in range(slabs):
-            remote = received(rows.start, LAST_CHUNK, slabs + slab)
-            total = kinetic[slab] + remote + potential_ref[slab, rows] * fields[slab][rows]
+    matrices = build_local(bond_ref, bend_ref, torsion_ref, umbrella_ref)
+    for rows, kinetic in local_kinetic(next_held, along_ref, *matrices):
+        for slab in range(slabs):
+            remote = received(rows.start, BLOCK, slabs + slab)
+            total = kinetic[slab] + remote + potential_ref[slab, rows] * next_held[slab, rows]
             factor = damping[slab][rows]
             last_held[slab, rows] = factor * (2.0 * total - factor * curr_ref[slab, rows])
-            part = pl.ds(rows.start, LAST_CHUNK)
-            sends.append(
-                pltpu.make_async_copy(last_held.at[slab, part], last_ref.at[slab, part], left.at[len(sends)])
-            )
-            sends[-1].start()
+        part = pl.ds(rows.start, BLOCK)
+        sends.append(
+            pltpu.make_async_copy(last_held.at[:, part], last_ref.at[:, part], left.at[len(sends)])
+        )
+        sends[-1].start()
     for send in sends:
         send.wait()
 
@@ -299,20 +314,14 @@
     )
     whole = pl.BlockSpec(memory_space=pltpu.VMEM)
     remote = pl.BlockSpec(memory_space=pltpu.HBM)
-    chunks = size // LAST_CHUNK
-    message, *matrices = pl.pallas_call(
+    held = pltpu.VMEM(flat, F32)
+    message = pl.pallas_call(
         lambda *refs: first_kernel(len(sources), *refs),
-        out_shape=(
-            shaped(size * stride, lanes),
-            shaped(size, size, dtype=BF16),
-            shaped(size, size, dtype=BF16),
-            shaped(2 * lanes, lanes, dtype=BF16),
-            shaped(lanes, lanes, dtype=BF16),
-        ),
+        out_shape=shaped(size * stride, lanes),
         in_specs=[remote] * len(sources),
-        out_specs=[whole] * 5,
+        out_specs=whole,
         scratch_shapes=[pltpu.VMEM(source.shape, F32) for source in sources]
-        + [pltpu.SemaphoreType.DMA((len(sources),))],
+        + [held, pltpu.SemaphoreType.DMA((len(sources),))],
         compiler_params=params(32),
     )(*sources)
     message = lax.all_to_all(
@@ -338,9 +347,9 @@
         out_shape=(shaped(*flat), shaped(*flat)),
         in_specs=[whole] * 8,
         out_specs=(remote, remote),
-        scratch_shapes=[pltpu.VMEM(flat, F32)] * 2 + [pltpu.SemaphoreType.DMA((1 + slabs * chunks,))],
+        scratch_shapes=[held] * 3 + [pltpu.SemaphoreType.DMA((1 + slabs * (size // BLOCK),))],
         compiler_params=params(32),
-    )(back, curr, field, damping, *matrices)
+    )(back, curr, field, damping, *inner)
     return next_term.reshape(packet_curr.shape), last_term.reshape(packet_curr.shape)
 
 

time: 108 us -> 107 us (level)
  no operation moved by 1% of the time
where the time goes in v5:
time: 107 us
  blocking collectives  101 us (94%)
  Pallas kernels  5.2 us (5%)
    all_to_all x1, blocking collectives, local(): lax.all_to_all(message.reshape(size, stride, 1, lanes), AXES, split_axis=...  61.7 us
    all_to_all x1, blocking collectives, local(): lax.all_to_all(back.reshape(size, 2 * slabs, lanes), AXES, split_axis=0,...  39.3 us

profile of v5, /device:TPU:1, one launch (start us, length us, event | category | flops | bytes accessed | tf_op | source)
XLA Modules:
  0.0 106.9 jit_solution(16567073439700607353)
XLA Ops:
  0.6 2.1 %shard_map.113 = f32[2560,128]{1,0:T(8,128)S(1)} custom-call(f32[32,32]{1,0:T(8,128)} %refs_4_.3, f32[16,16]{1,0:T(8,128)} %refs_5_.1, f32[16,16]{1,0:T(8,128)} %refs_6_.1, f32[8,8]{1,0:T(8,128)} %refs_7_.1, f32[2,32]{1,0:T(2,128)} %refs_3_.3, f32[2,512,128]{2,1,0:T(8,128)} %bitcast.17, f32[2,512,128]{2,1,0:T(8,128)} %bitcast.19, f32[2,512,128]{2,1,0:T(8,128)} %bitcast.21), custom_call_target="tpu_custom_call" | custom-call | tf_op jit(solution)/shard_map/pallas_call | solution.py:318
  2.7 0.0 copy-start.3
  2.7 0.0 copy-start.7
  2.7 61.7 %all_to_all.10 = f32[512,5,1,128]{3,2,1,0:T(1,128)S(1)} all-to-all(f32[512,5,1,128]{3,2,1,0:T(1,128)S(1)} %bitcast.14), channel_id=1, replica_groups=mesh['wide'=32,'narrow'=16] {'wide','narrow'}, dimensions={0} | all-to-all | bytes 2621440 | tf_op jit(solution)/shard_map/all_to_all | solution.py:327
  64.4 0.0 copy-done.3
  64.4 0.0 copy-done.7
  64.4 1.3 %shard_map.114 = f32[2048,128]{1,0:T(8,128)S(1)} custom-call(f32[2560,128]{1,0:T(8,128)S(1)} %bitcast.13, f32[64,64]{1,0:T(8,128)S(1)} %copy-done.3, f32[16,16]{1,0:T(8,128)S(1)} %copy-done.7), custom_call_target="tpu_custom_call" | custom-call | tf_op jit(solution)/shard_map/pallas_call | solution.py:331
  65.7 0.0 copy-start
  65.7 0.0 copy-start.1
  65.7 0.0 copy-start.2
  65.8 0.0 copy-start.4
  65.8 0.0 copy-start.5
  65.8 0.0 copy-start.6
  65.8 0.0 copy-start.8
  65.8 39.3 %all_to_all.11 = f32[512,4,128]{2,1,0:T(4,128)S(1)} all-to-all(f32[512,4,128]{2,1,0:T(4,128)S(1)} %bitcast.15), channel_id=1, replica_groups={{448,464,449,465,450,466,451,467,452,468,453,469,454,470,455,471,456,47..., dimensions={0} | all-to-all | bytes 2097152 | tf_op jit(solution)/shard_map/all_to_all | solution.py:337
  105.1 0.0 copy-done
  105.1 0.0 copy-done.1
  105.1 0.0 copy-done.2
  105.1 0.0 copy-done.4
  105.1 0.0 copy-done.5
  105.1 0.0 copy-done.6
  105.1 0.0 copy-done.8
  105.1 1.8 %shard_map.115 = (f32[2,512,128]{2,1,0:T(8,128)}, f32[2,512,128]{2,1,0:T(8,128)}) custom-call(f32[2048,128]{1,0:T(8,128)S(1)} %bitcast.16, f32[2,512,128]{2,1,0:T(8,128)S(1)} %bitcast.18, f32[2,512,128]{2,1,0:T(8,128)S(1)} %bitcast.20, f32[2,32]{1,0:T(2,128)S(1)} %copy-done.8, f32[32,32]{1,0:T(8,128)S(1)} %copy-done.2, f32[16,16]{1,0:T(8,128)S(1)} %copy-done.4, ...), custom_call_target="tpu_custom_call" | custom-call | tf_op jit(solution)/shard_map/pallas_call | solution.py:345
Async XLA Ops:
  2.7 61.7 %copy-start.3 = (f32[64,64]{1,0:T(8,128)S(1)}, f32[64,64]{1,0:T(8,128)}, u32[]{:S(2)}) copy-start(f32[64,64]{1,0:T(8,128)} %refs_1_.3) | copy-start | bytes 49156
  2.7 61.7 %copy-start.7 = (f32[16,16]{1,0:T(8,128)S(1)}, f32[16,16]{1,0:T(8,128)}, u32[]{:S(2)}) copy-start(f32[16,16]{1,0:T(8,128)} %refs_2_.3) | copy-start | bytes 3076
  65.7 39.3 %copy-start = (f32[2,512,1,128]{3,2,1,0:T(1,128)S(1)}, f32[2,512,1,128]{3,2,1,0:T(1,128)}, u32[]{:S(2)}) copy-start(f32[2,512,1,128]{3,2,1,0:T(1,128)} %param.11) | copy-start | bytes 1572868
  65.7 39.3 %copy-start.1 = (f32[2,512,1,128]{3,2,1,0:T(1,128)S(1)}, f32[2,512,1,128]{3,2,1,0:T(1,128)}, u32[]{:S(2)}) copy-start(f32[2,512,1,128]{3,2,1,0:T(1,128)} %param.12) | copy-start | bytes 1572868
  65.7 39.3 %copy-start.2 = (f32[32,32]{1,0:T(8,128)S(1)}, f32[32,32]{1,0:T(8,128)}, u32[]{:S(2)}) copy-start(f32[32,32]{1,0:T(8,128)} %refs_4_.3) | copy-start | bytes 12292
  65.8 39.3 %copy-start.4 = (f32[16,16]{1,0:T(8,128)S(1)}, f32[16,16]{1,0:T(8,128)}, u32[]{:S(2)}) copy-start(f32[16,16]{1,0:T(8,128)} %refs_5_.1) | copy-start | bytes 3076
  65.8 39.3 %copy-start.5 = (f32[16,16]{1,0:T(8,128)S(1)}, f32[16,16]{1,0:T(8,128)}, u32[]{:S(2)}) copy-start(f32[16,16]{1,0:T(8,128)} %refs_6_.1) | copy-start | bytes 3076
  65.8 39.3 %copy-start.6 = (f32[8,8]{1,0:T(8,128)S(1)}, f32[8,8]{1,0:T(8,128)}, u32[]{:S(2)}) copy-start(f32[8,8]{1,0:T(8,128)} %refs_7_.1) | copy-start | bytes 772
  65.8 39.3 %copy-start.8 = (f32[2,32]{1,0:T(2,128)S(1)}, f32[2,32]{1,0:T(2,128)}, u32[]{:S(2)}) copy-start(f32[2,32]{1,0:T(2,128)} %refs_3_.3) | copy-start | bytes 772
